TPU v7x, 32 devices: a whole 2x2x4 slice. The times are simulated.
32 devices in a mesh: dp: 8 (over z, x), row: 2 (over y), col: 2 (over core).
Axes of the slice: x: 2, y: 2, z: 4, core: 2. Of those that a mesh axis runs over, the one named last changes fastest.
Arguments:
- tokens: bfloat16 [2048, 896], P(('dp', 'row'), 'col'), may hold values from -6 to 6
- seq_lengths: int32 [8, 3], P('dp'), may hold values from 1 to 160, 256 in all within a row
- cotangent: bfloat16 [2048, 896], P(('dp', 'row'), 'col'), may hold values from -6 to 6
- norm1_gain: float32 [896], P('col'), may hold values from 0.5 to 1.5
- q_weight: bfloat16 [896, 896], P('col', 'row'), may hold values from -0.1875 to 0.1875
- q_bias: float32 [896], P('row'), may hold values from -3 to 3
- k_weight: bfloat16 [896, 128], P('col', 'row'), may hold values from -0.1875 to 0.1875
- k_bias: float32 [128], P('row'), may hold values from -3 to 3
- v_weight: bfloat16 [896, 128], P('col', 'row'), may hold values from -0.1875 to 0.1875
- v_bias: float32 [128], P('row'), may hold values from -0.6 to 0.6
- o_weight: bfloat16 [896, 896], P('row', 'col'), may hold values from -1.5 to 1.5
- norm2_gain: float32 [896], P('col'), may hold values from 0.5 to 1.5
- gate_weight: bfloat16 [896, 4864], P('col', 'row'), may hold values from -0.1875 to 0.1875
- up_weight: bfloat16 [896, 4864], P('col', 'row'), may hold values from -0.1875 to 0.1875
- down_weight: bfloat16 [4864, 896], P('row', 'col'), may hold values from -0.078125 to 0.078125
Outputs:
- output: bfloat16 [2048, 896], P(('dp', 'row'), 'col')
- input_grad: bfloat16 [2048, 896], P(('dp', 'row'), 'col')
- norm1_gain_grad: float32 [896], P('col')
- q_weight_grad: float32 [896, 896], P(('col', 'dp'), 'row')
- q_bias_grad: float32 [896], P('row')
- k_weight_grad: float32 [896, 128], P(('col', 'dp'), 'row')
- k_bias_grad: float32 [128], P('row')
- v_weight_grad: float32 [896, 128], P(('col', 'dp'), 'row')
- v_bias_grad: float32 [128], P('row')
- o_weight_grad: float32 [896, 896], P(('row', 'dp'), 'col')
- norm2_gain_grad: float32 [896], P('col')
- gate_weight_grad: float32 [896, 4864], P(('col', 'dp'), 'row')
- up_weight_grad: float32 [896, 4864], P(('col', 'dp'), 'row')
- down_weight_grad: float32 [4864, 896], P(('row', 'dp'), 'col')
Inputs may be any that keep to these rules, and one draw needn't show every extreme that they name: `seq_lengths`: in each data group the 3 lengths add up to 256, and the longest is exactly 160.
All inputs are finite; a program needn't handle non-finite values.
Results may differ from a plain program's by a relative error of at most 0.029.
Values may be sent and summed in bfloat16 or wider, within the bound.
A program may use at most 128 MiB of HBM per device.

v0:
```python
import jax
import jax.numpy as jnp
from jax import lax
from jax.sharding import PartitionSpec as P

D = 896
HD = 64


NEGATIVE = -1e30
EPSILON = 1e-06
ROTARY_BASE = 1000000.0


def sequence_tables(lengths, group_rows):
    seq_ends = jnp.cumsum(lengths)
    seq_starts = seq_ends - lengths
    places = jnp.arange(group_rows, dtype=jnp.int32)
    segment = jnp.sum((places[:, None] >= seq_ends[None, :]).astype(jnp.int32), axis=1)
    member = segment[:, None] == jnp.arange(lengths.shape[0], dtype=jnp.int32)[None, :]
    position = places - jnp.sum(jnp.where(member, seq_starts[None, :], 0), axis=1)
    return (places, segment, position)


def rotary_tables(position):
    half_width = HD // 2
    frequency = ROTARY_BASE ** (-(jnp.arange(half_width, dtype=jnp.float32) * 2.0 / HD))
    angle = position.astype(jnp.float32)[:, None] * frequency[None, :]
    cosine = jnp.cos(angle)
    sine = jnp.sin(angle)
    return (
        jnp.concatenate([cosine, cosine], 1)[:, None, :],
        jnp.concatenate([sine, sine], 1)[:, None, :],
    )


def rotary(values, cosine, sine):
    half_width = values.shape[-1] // 2
    turned = jnp.concatenate([-values[..., half_width:], values[..., :half_width]], -1)
    return values * cosine + turned * sine


def rotary_back(gradient, cosine, sine):
    turned = gradient * sine
    half_width = turned.shape[-1] // 2
    return gradient * cosine + jnp.concatenate(
        [turned[..., half_width:], -turned[..., :half_width]], -1
    )


def feature_total(values):
    return lax.psum(values, "col")


def norm_forward(values, gain_vector):
    inverse = lax.rsqrt(feature_total(jnp.sum(values * values, axis=1)) / D + EPSILON)
    return ((values * inverse[:, None] * gain_vector).astype(jnp.bfloat16), inverse)


def norm_backward(gradient, values, inverse, gain_vector):
    weighted = gradient * gain_vector
    column_total = feature_total(jnp.sum(weighted * values, axis=1))
    back_value = (
        weighted * inverse[:, None]
        - values * (inverse * inverse * inverse * column_total / D)[:, None]
    )
    return (back_value, jnp.sum(gradient * values * inverse[:, None], axis=0))


def spread_rows(values):
    return lax.all_gather(values, "row", axis=0, tiled=True)


def spread_cols(values):
    return lax.all_gather(values, "col", axis=0, tiled=True)


def product(left_side, weight, flipped):
    if flipped:
        return lax.dot_general(
            left_side, weight, (((1,), (1,)), ((), ())), preferred_element_type=jnp.float32
        )
    return jnp.dot(left_side, weight, preferred_element_type=jnp.float32)


def outer_sum(left_side, right_side):
    return lax.dot_general(
        left_side, right_side, (((0,), (0,)), ((), ())), preferred_element_type=jnp.float32
    )


def data_total(left_side, right_side):
    return lax.psum_scatter(outer_sum(left_side, right_side), "dp", scatter_dimension=0, tiled=True)


def across_columns(gathered, weight, flipped, row_count):

    def partial_term(first_row, how_many):
        return product(gathered, weight, flipped)

    return lax.psum_scatter(
        partial_term(jnp.int32(0), lax.axis_size("col") * row_count),
        "col",
        scatter_dimension=0,
        tiled=True,
    )


def across_rows(gathered, weight, flipped, row_count):

    def partial_term(first_row, how_many):
        return product(gathered, weight, flipped)

    return lax.psum_scatter(
        partial_term(jnp.int32(0), lax.axis_size("row") * row_count),
        "row",
        scatter_dimension=0,
        tiled=True,
    )


def per_device(
    tokens,
    seq_lengths,
    cotangent,
    norm1_gain,
    q_weight,
    q_bias,
    k_weight,
    k_bias,
    v_weight,
    v_bias,
    o_weight,
    norm2_gain,
    gate_weight,
    up_weight,
    down_weight,
):
    local_rows = tokens.shape[0]
    group_rows = local_rows * lax.axis_size("row")
    head_rows = group_rows // lax.axis_size("col")
    query_width = q_weight.shape[1]
    key_width = k_weight.shape[1]
    query_heads = query_width // HD
    value_heads = key_width // HD
    hidden_width = gate_weight.shape[1]
    score_scale = HD ** (-0.5)
    places, segment, position = sequence_tables(seq_lengths[0], group_rows)
    block_start = lax.axis_index("col") * head_rows
    own_places = lax.dynamic_slice_in_dim(places, block_start, head_rows, 0)
    own_segment = lax.dynamic_slice_in_dim(segment, block_start, head_rows, 0)
    own_position = lax.dynamic_slice_in_dim(position, block_start, head_rows, 0)
    allowed = (own_segment[:, None] == segment[None, :]) & (places[None, :] <= own_places[:, None])
    cosine, sine = rotary_tables(own_position)
    inputs = tokens.astype(jnp.float32)
    normed1, inverse1 = norm_forward(inputs, norm1_gain)
    normed1_all = spread_rows(normed1)
    joint_weight = jnp.concatenate([q_weight, k_weight, v_weight], axis=1)
    joint_bias = jnp.concatenate([q_bias, k_bias, v_bias])
    projected = across_columns(normed1_all, joint_weight, False, head_rows) + joint_bias
    queries = rotary(
        projected[:, :query_width].reshape(head_rows, query_heads, HD), cosine, sine
    ).astype(jnp.bfloat16)
    keys_local = rotary(
        projected[:, query_width : query_width + key_width].reshape(head_rows, value_heads, HD),
        cosine,
        sine,
    ).astype(jnp.bfloat16)
    values_local = (
        projected[:, query_width + key_width :]
        .reshape(head_rows, value_heads, HD)
        .astype(jnp.bfloat16)
    )
    keys_all, values_all = (
        lax.all_gather(keys_local, "col", axis=0, tiled=True),
        lax.all_gather(values_local, "col", axis=0, tiled=True),
    )
    grouped = queries.reshape(head_rows, value_heads, query_heads // value_heads, HD)

    def score_table():
        raw_scores = (
            jnp.einsum("tkgd,skd->kgts", grouped, keys_all, preferred_element_type=jnp.float32)
            * score_scale
        )
        return jnp.where(allowed[None, None], raw_scores, NEGATIVE)

    scores = score_table()
    highest = jnp.max(scores, axis=-1, keepdims=True)
    raised = jnp.exp(scores - highest)
    row_total = jnp.sum(raised, axis=-1, keepdims=True)
    log_total = highest + jnp.log(row_total)
    probs = (raised / row_total).astype(jnp.bfloat16)
    mixed = jnp.einsum("kgts,skd->tkgd", probs, values_all, preferred_element_type=jnp.float32)
    mixed = mixed.reshape(head_rows, query_width).astype(jnp.bfloat16)
    mixed_all = spread_cols(mixed)
    attention = across_rows(mixed_all, o_weight, False, local_rows)
    hidden = inputs + attention
    normed2, inverse2 = norm_forward(hidden, norm2_gain)
    normed2_all = spread_rows(normed2)
    gate_up = jnp.concatenate([gate_weight, up_weight], axis=1)
    both_values = across_columns(normed2_all, gate_up, False, head_rows)
    gate_value = both_values[:, :hidden_width]
    up_value = both_values[:, hidden_width:]
    sigmoid_value = jax.nn.sigmoid(gate_value)
    silu_value = gate_value * sigmoid_value
    activated = (silu_value * up_value).astype(jnp.bfloat16)
    activated_all = spread_cols(activated)
    feed_forward = across_rows(activated_all, down_weight, False, local_rows)
    output = (hidden + feed_forward).astype(jnp.bfloat16)
    grad_output_all = spread_rows(cotangent)
    grad_activated = across_columns(grad_output_all, down_weight, True, head_rows)
    grad_gate = (
        grad_activated * up_value * (sigmoid_value * (1.0 + gate_value * (1.0 - sigmoid_value)))
    )
    grad_up = grad_activated * silu_value
    grad_both = jnp.concatenate([grad_gate, grad_up], axis=1).astype(jnp.bfloat16)
    grad_both_all = spread_cols(grad_both)
    grad_normed2 = across_rows(grad_both_all, gate_up, True, local_rows)
    back_second, gain2_part = norm_backward(grad_normed2, hidden, inverse2, norm2_gain)
    grad_hidden = cotangent.astype(jnp.float32) + back_second
    grad_branch_all = spread_rows(grad_hidden.astype(jnp.bfloat16))
    grad_mixed = across_columns(grad_branch_all, o_weight, True, head_rows).astype(jnp.bfloat16)
    grad_grouped = grad_mixed.reshape(head_rows, value_heads, query_heads // value_heads, HD)
    probs_again = jnp.exp(score_table() - log_total)
    grad_probs = jnp.einsum(
        "tkgd,skd->kgts", grad_grouped, values_all, preferred_element_type=jnp.float32
    )
    grad_scores = probs_again * (
        grad_probs - jnp.sum(grad_probs * probs_again, axis=-1, keepdims=True)
    )
    grad_scores = grad_scores.astype(jnp.bfloat16)
    grad_queries = (
        jnp.einsum("kgts,skd->tkgd", grad_scores, keys_all, preferred_element_type=jnp.float32)
        * score_scale
    )
    grad_keys_part = (
        jnp.einsum("kgts,tkgd->skd", grad_scores, grouped, preferred_element_type=jnp.float32)
        * score_scale
    )
    grad_values_part = jnp.einsum(
        "kgts,tkgd->skd",
        probs_again.astype(jnp.bfloat16),
        grad_grouped,
        preferred_element_type=jnp.float32,
    )
    grad_keys, grad_values = (
        lax.psum_scatter(
            grad_keys_part.astype(jnp.bfloat16), "col", scatter_dimension=0, tiled=True
        ).astype(jnp.float32),
        lax.psum_scatter(
            grad_values_part.astype(jnp.bfloat16), "col", scatter_dimension=0, tiled=True
        ).astype(jnp.float32),
    )
    grad_q = rotary_back(grad_queries.reshape(head_rows, query_heads, HD), cosine, sine).reshape(
        head_rows, query_width
    )
    grad_k = rotary_back(grad_keys, cosine, sine).reshape(head_rows, key_width)
    grad_v = grad_values.reshape(head_rows, key_width)
    grad_projected = jnp.concatenate([grad_q, grad_k, grad_v], axis=1).astype(jnp.bfloat16)
    grad_projected_all = spread_cols(grad_projected)
    bias_part = jnp.sum(grad_projected_all, axis=0, dtype=jnp.float32)
    grad_normed1 = across_rows(grad_projected_all, joint_weight, True, local_rows)
    back_first, gain1_part = norm_backward(grad_normed1, inputs, inverse1, norm1_gain)
    input_grad = (grad_hidden + back_first).astype(jnp.bfloat16)
    gain1_final, gain2_final = lax.psum((gain1_part, gain2_part), ("dp", "row"))
    qbias_final, kbias_final, vbias_final = lax.psum(
        (
            bias_part[:query_width],
            bias_part[query_width : query_width + key_width],
            bias_part[query_width + key_width :],
        ),
        "dp",
    )
    down_final = data_total(activated_all, grad_output_all)
    gate_up_final = data_total(normed2_all, grad_both_all)
    output_final = data_total(mixed_all, grad_branch_all)
    joint_final = data_total(normed1_all, grad_projected_all)
    query_final = joint_final[:, :query_width]
    key_final = joint_final[:, query_width : query_width + key_width]
    value_final = joint_final[:, query_width + key_width :]
    gate_final = gate_up_final[:, :hidden_width]
    up_final = gate_up_final[:, hidden_width:]
    return (
        output,
        input_grad,
        gain1_final,
        query_final,
        qbias_final,
        key_final,
        kbias_final,
        value_final,
        vbias_final,
        output_final,
        gain2_final,
        gate_final,
        up_final,
        down_final,
    )


def solution(mesh):
    placed = (
        P(("dp", "row"), "col"),
        P("dp", None),
        P(("dp", "row"), "col"),
        P("col"),
        P("col", "row"),
        P("row"),
        P("col", "row"),
        P("row"),
        P("col", "row"),
        P("row"),
        P("row", "col"),
        P("col"),
        P("col", "row"),
        P("col", "row"),
        P("row", "col"),
    )
    return jax.shard_map(
        per_device,
        mesh=mesh,
        in_specs=placed,
        out_specs=(
            P(("dp", "row"), "col"),
            P(("dp", "row"), "col"),
            P("col"),
            P(("col", "dp"), "row"),
            P("row"),
            P(("col", "dp"), "row"),
            P("row"),
            P(("col", "dp"), "row"),
            P("row"),
            P(("row", "dp"), "col"),
            P("col"),
            P(("col", "dp"), "row"),
            P(("col", "dp"), "row"),
            P(("row", "dp"), "col"),
        ),
        check_vma=False,
    )
```

profile of v0, /device:TPU:0, one launch (start us, length us, event | category | flops | bytes accessed | tf_op | source)
XLA Modules:
  0.0 636.7 jit_solution(3044601873346287037)
XLA Ops:
  7.2 1.1 fusion.19
  8.4 2.6 psum.63
  10.9 1.0 copy.41
  11.9 1.0 copy.42
  13.0 1.1 fusion.21
  14.1 7.0 %all_gather.30 = bf16[256,448]{0,1:T(8,128)(2,1)S(1)} all-gather(bf16[128,448]{0,1:T(8,128)(2,1)S(1)} %fusion.21), channel_id=1, replica_groups=mesh['dp'=8,'row'=2,'col'=2] {'row'}, dimensions={0}, use_global_device_ids=true | all-gather | bytes 344064 | tf_op jit(solution)/shard_map/all_gather | solution.py:71
  21.1 2.5 fusion.29
  24.7 8.6 %reduce-scatter.18.cloned.1.call-done = f32[128,576]{0,1:T(8,128)} async-done(((f32[256,576]{0,1:T(8,128)}), f32[128,576]{0,1:T(8,128)}) %reduce-scatter.18.cloned.1.call-update) | async-done | bytes 294928 | tf_op jit(solution)/shard_map/reduce_scatter | solution.py:101
  33.3 1.1 broadcast_add_fusion
  34.5 1.8 all-gather
  36.3 1.8 all-gather.1
  39.7 2.1 all_gather.33
  41.8 1.1 fusion.56
  43.0 6.0 all_gather.36
  49.7 2.3 fusion.59
  52.1 3.3 constant_dynamic-update-slice_fusion.1
  55.4 1.6 constant_dynamic-update-slice_fusion
  57.0 1.0 reduce-scatter.20.cloned.1.call-done
  58.1 1.5 multiply_reduce_fusion.3
  59.6 3.1 psum.64
  63.8 0.8 multiply_convert_fusion.4
  64.6 6.0 all_gather.34
  71.3 5.9 fusion.57
  77.3 13.1 %reduce-scatter.22.cloned.1.call-done = f32[128,4864]{1,0:T(8,128)} async-done(((f32[256,4864]{1,0:T(8,128)}), f32[128,4864]{1,0:T(8,128)}) %reduce-scatter.22.cloned.1.call-update) | async-done | bytes 2490384 | tf_op jit(solution)/shard_map/reduce_scatter | solution.py:101
  90.4 3.5 multiply_convert_fusion.1
  94.0 1.1 pad_maximum_fusion
  95.2 12.5 %all-gather.7.cloned.1.call-done = bf16[256,4864]{1,0:T(8,128)(2,1)} async-done(((bf16[128,4864]{1,0:T(8,128)(2,1)}), bf16[256,4864]{1,0:T(8,128)(2,1)}) %all-gather.7.cloned.1.call-update) | async-done | bytes 2490384 | tf_op jit(solution)/shard_map/all_gather | solution.py:75
  107.7 5.1 fusion.60
  112.8 15.1 %reduce-scatter.28.cloned.1.call-done = f32[128,448]{0,1:T(8,128)} async-done(((f32[256,448]{0,1:T(8,128)}), f32[128,448]{0,1:T(8,128)}) %reduce-scatter.28.cloned.1.call-update) | async-done | bytes 229392 | tf_op jit(solution)/shard_map/reduce_scatter | solution.py:114
  127.9 1.7 multiply_reduce_fusion.1
  129.7 3.1 psum.65
  133.5 1.1 fusion.49
  134.6 5.9 all_gather.38
  141.2 1.0 fusion.65
  142.4 7.9 %reduce-scatter.30.cloned.1.call-done = f32[128,448]{0,1:T(8,128)} async-done(((f32[256,448]{0,1:T(8,128)}), f32[128,448]{0,1:T(8,128)}) %reduce-scatter.30.cloned.1.call-update) | async-done | bytes 229392 | tf_op jit(solution)/shard_map/reduce_scatter | solution.py:101
  150.3 1.0 convert_element_type.121
  151.6 1.3 multiply_reduce_fusion
  153.7 1.4 fusion.12
  157.6 1.2 bitcast_multiply_fusion.2
  159.0 3.4 reduce-scatter.42.cloned.1.call-done
  162.4 0.8 copy.58
  163.2 10.6 %reduce-scatter.40.cloned.1.call-done = bf16[128,64]{1,0:T(8,128)(2,1)} async-done(((bf16[256,64]{1,0:T(8,128)(2,1)}), bf16[128,64]{1,0:T(8,128)(2,1)}) %reduce-scatter.40.cloned.1.call-update) | async-done | bytes 16400
  173.8 0.8 copy.56
  174.7 2.0 all_gather.39
  176.7 2.2 fusion.28
  179.0 7.3 %all-gather.5.cloned.1.call-done = bf16[256,2432]{1,0:T(8,128)(2,1)} async-done(((bf16[128,2432]{1,0:T(8,128)(2,1)}), bf16[256,2432]{1,0:T(8,128)(2,1)}) %all-gather.5.cloned.1.call-update) | async-done | bytes 1245200 | tf_op jit(solution)/shard_map/all_gather | solution.py:75
  186.3 2.9 fusion.58
  189.2 1.4 fusion.61
  190.9 6.4 %fusion.63 = f32[448,4864]{1,0:T(8,128)} fusion(bf16[256,448]{0,1:T(8,128)(2,1)S(1)} %copy-done.4, bf16[256,4864]{1,0:T(8,128)(2,1)} %all-gather.7.cloned.1.call-done), kind=kOutput, calls=%fused_computation.132 | convolution fusion | flops 1115684864 | bytes 11436032 | tf_op jit(solution)/shard_map/dot_general | solution.py:87
  197.4 0.8 copy-done.12
  198.3 1.3 fusion.62
  199.7 4.5 fusion.64
  206.3 22.2 %all-reduce.2 = (f32[448]{0:T(512)}, f32[64]{0:T(128)}, f32[64]{0:T(128)}) all-reduce(f32[448]{0:T(512)S(1)} %slice.78, f32[64]{0:T(128)S(1)} %get-tuple-element.46, f32[64]{0:T(128)S(1)} %get-tuple-element.45), channel_id=1, replica_groups=mesh['dp'=8,'row'=2,'col'=2] {'dp'}, use_global_device_ids=true, to_apply=%region_28.29 | all-reduce | flops 576 | bytes 4608 | tf_op jit(solution)/shard_map/psum | solution.py:266
  228.5 1.2 fusion.27
  229.6 2.5 psum.66
  232.1 38.9 %all-reduce.1 = (f32[448]{0:T(512)}, f32[448]{0:T(512)}) all-reduce(f32[448]{0:T(512)S(1)} %get-tuple-element.16, f32[448]{0:T(512)S(1)} %copy-done.45), channel_id=1, replica_groups=mesh['dp'=8,'row'=2,'col'=2] {'dp','row'}, use_global_device_ids=true, to_apply=%region_25.26 | all-reduce | flops 896 | bytes 7168 | tf_op jit(solution)/shard_map/psum | solution.py:265
  271.1 1.9 fusion.25
  272.9 31.4 %all-reduce.5.cloned.1.call-done = f32[448,576]{1,0:T(8,128)} async-done(((f32[448,576]{1,0:T(8,128)}), f32[448,576]{1,0:T(8,128)}) %all-reduce.5.cloned.1.call-update) | async-done | bytes 1032208
  304.3 1.6 fusion.50
  305.9 1.6 constant_dynamic-slice_fusion
  307.5 154.3 %reduce-scatter.36.cloned.1.call-done = f32[56,4864]{1,0:T(8,128)} async-done(((f32[448,4864]{1,0:T(8,128)}), f32[56,4864]{1,0:T(8,128)}) %reduce-scatter.36.cloned.1.call-update) | async-done | bytes 1089552 | tf_op jit(solution)/shard_map/reduce_scatter | solution.py:93
  461.8 2.3 fusion.51
  464.0 63.9 %reduce-scatter.34.cloned.1.call-done = f32[56,448]{1,0:T(8,128)} async-done(((f32[448,448]{1,0:T(8,128)}), f32[56,448]{1,0:T(8,128)}) %reduce-scatter.34.cloned.1.call-update) | async-done | bytes 100368 | tf_op jit(solution)/shard_map/reduce_scatter | solution.py:93
  527.9 102.2 %reduce-scatter.38.cloned.1.call-done = f32[304,448]{1,0:T(8,128)} async-done(((f32[2432,448]{1,0:T(8,128)}), f32[304,448]{1,0:T(8,128)}) %reduce-scatter.38.cloned.1.call-update) | async-done | bytes 544784 | tf_op jit(solution)/shard_map/reduce_scatter | solution.py:93
  (196 shorter events, 12.7 us)
Async XLA Ops:
  7.2 42.6 %copy-start = (bf16[2432,448]{0,1:T(8,128)(2,1)S(1)}, bf16[2432,448]{0,1:T(8,128)(2,1)}, u32[]{:S(2)}) copy-start(bf16[2432,448]{0,1:T(8,128)(2,1)} %param.29) | copy-start | bytes 6537220
  7.2 26.1 %reduce-scatter.18.cloned.1.call-start = ((), (), s32[]{:S(2)}) async-start(), calls=%async_computation.13 | async-start | bytes 884736 | tf_op jit(solution)/shard_map/reduce_scatter | solution.py:101
  10.9 2.0 copy-start.56
  10.9 2.0 copy-start.48
  11.9 11.7 %copy-start.35 = (bf16[448,64]{1,0:T(8,128)(2,1)}, bf16[448,64]{1,0:T(8,128)(2,1)S(1)}, u32[]{:S(2)}) copy-start(bf16[448,64]{1,0:T(8,128)(2,1)S(1)} %copy.41) | copy-start | bytes 172036
  13.0 10.6 %copy-start.37 = (bf16[448,64]{1,0:T(8,128)(2,1)}, bf16[448,64]{1,0:T(8,128)(2,1)S(1)}, u32[]{:S(2)}) copy-start(bf16[448,64]{1,0:T(8,128)(2,1)S(1)} %copy.42) | copy-start | bytes 172036
  21.1 2.5 copy-start.21
  21.1 2.6 copy-start.55
  21.1 3.2 copy-start.50
  21.1 3.2 copy-start.53
  21.1 3.2 copy-start.54
  23.6 34.4 %reduce-scatter.20.cloned.1.call-start = ((), (), s32[]{:S(2)}) async-start(), calls=%async_computation.14 | async-start | bytes 688128 | tf_op jit(solution)/shard_map/reduce_scatter | solution.py:114
  24.5 13.7 %copy-start.29 = (f32[128,32]{0,1:T(8,128)}, f32[128,32]{0,1:T(8,128)S(1)}, u32[]{:S(2)}) copy-start(f32[128,32]{0,1:T(8,128)S(1)} %get-tuple-element.47) | copy-start | bytes 49156
  24.5 13.7 %copy-start.31 = (f32[128,32]{0,1:T(8,128)}, f32[128,32]{0,1:T(8,128)S(1)}, u32[]{:S(2)}) copy-start(f32[128,32]{0,1:T(8,128)S(1)} %get-tuple-element.48) | copy-start | bytes 49156
  34.5 4.2 copy-start.6
  36.3 2.8 copy-start.33
  36.3 2.3 copy-start.23
  36.3 2.3 copy-start.27
  39.1 2.7 copy-start.17
  39.7 3.3 copy-start.19
  41.8 10.3 %copy-start.11 = (bf16[256,448]{0,1:T(8,128)(2,1)}, bf16[256,448]{0,1:T(8,128)(2,1)S(1)}, u32[]{:S(2)}) copy-start(bf16[256,448]{0,1:T(8,128)(2,1)S(1)} %all_gather.33) | copy-start | bytes 688132
  42.9 34.4 %reduce-scatter.26.cloned.1.call-start = ((), (), s32[]{:S(2)}) async-start(), calls=%async_computation.18 | async-start | bytes 3735552 | tf_op jit(solution)/shard_map/reduce_scatter | solution.py:101
  52.1 38.4 %reduce-scatter.22.cloned.1.call-start = ((), (), s32[]{:S(2)}) async-start(), calls=%async_computation.15 | async-start | bytes 7471104 | tf_op jit(solution)/shard_map/reduce_scatter | solution.py:101
  52.1 3.3 copy-start.5
  55.4 2.6 copy-start.2
  77.2 30.4 %all-gather.7.cloned.1.call-start = ((), (), s32[]{:S(2)}) async-start(), calls=%async_computation.19 | async-start | bytes 3735552 | tf_op jit(solution)/shard_map/all_gather | solution.py:75
  95.1 32.8 %reduce-scatter.28.cloned.1.call-start = ((), (), s32[]{:S(2)}) async-start(), calls=%async_computation.20 | async-start | bytes 688128 | tf_op jit(solution)/shard_map/reduce_scatter | solution.py:114
  112.8 37.6 %reduce-scatter.30.cloned.1.call-start = ((), (), s32[]{:S(2)}) async-start(), calls=%async_computation.21 | async-start | bytes 688128 | tf_op jit(solution)/shard_map/reduce_scatter | solution.py:101
  132.8 8.5 %copy-start.18 = (bf16[448,448]{1,0:T(8,128)(2,1)S(1)}, bf16[448,448]{1,0:T(8,128)(2,1)}, u32[]{:S(2)}) copy-start(bf16[448,448]{1,0:T(8,128)(2,1)} %param.25) | copy-start | bytes 1204228
  133.5 7.0 %copy-start.51 = (f32[128]{0:T(128)}, f32[128]{0:T(128)S(1)}, u32[]{:S(2)}) copy-start(f32[128]{0:T(128)S(1)} %fusion.46) | copy-start | bytes 1540
  134.6 7.8 %copy-start.40 = (f32[7,128]{1,0:T(8,128)S(1)}, f32[7,128]{1,0:T(8,128)}, u32[]{:S(2)}) copy-start(f32[7,128]{1,0:T(8,128)} %copy-done.39) | copy-start | bytes 10756
  134.6 7.8 %copy-start.44 = (f32[7,128]{1,0:T(8,128)S(1)}, f32[7,128]{1,0:T(8,128)}, u32[]{:S(2)}) copy-start(f32[7,128]{1,0:T(8,128)} %copy-done.43) | copy-start | bytes 10756
  141.2 10.3 %copy-start.34 = (bf16[256,64]{0,1:T(8,128)(2,1)S(1)}, bf16[256,64]{0,1:T(8,128)(2,1)}, u32[]{:S(2)}) copy-start(bf16[256,64]{0,1:T(8,128)(2,1)} %copy-done.33) | copy-start | bytes 98308
  142.3 20.1 %reduce-scatter.42.cloned.1.call-start = ((), (), s32[]{:S(2)}) async-start(), calls=%async_computation.27 | async-start | bytes 98304
  152.8 3.0 copy-start.24
  153.6 20.2 %reduce-scatter.40.cloned.1.call-start = ((), (), s32[]{:S(2)}) async-start(), calls=%async_computation.26 | async-start | bytes 98304
  153.7 2.2 copy-start.7
  153.7 2.2 copy-start.10
  155.9 1.7 copy-start.26
  155.9 1.7 copy-start.28
  156.9 29.3 %all-gather.5.cloned.1.call-start = ((), (), s32[]{:S(2)}) async-start(), calls=%async_computation.16 | async-start | bytes 1867776 | tf_op jit(solution)/shard_map/all_gather | solution.py:75
  157.5 17.1 %copy-start.32 = (f32[128,32]{0,1:T(8,128)S(1)}, f32[128,32]{0,1:T(8,128)}, u32[]{:S(2)}) copy-start(f32[128,32]{0,1:T(8,128)} %copy-done.31) | copy-start | bytes 49156
  157.5 17.1 %copy-start.30 = (f32[128,32]{0,1:T(8,128)S(1)}, f32[128,32]{0,1:T(8,128)}, u32[]{:S(2)}) copy-start(f32[128,32]{0,1:T(8,128)} %copy-done.29) | copy-start | bytes 49156
  157.6 70.9 %reduce-scatter.32.cloned.1.call-start = ((), (), s32[]{:S(2)}) async-start(), calls=%async_computation.22 | async-start | bytes 688128 | tf_op jit(solution)/shard_map/reduce_scatter | solution.py:114
  158.9 17.9 %copy-start.36 = (bf16[448,64]{1,0:T(8,128)(2,1)S(1)}, bf16[448,64]{1,0:T(8,128)(2,1)}, u32[]{:S(2)}) copy-start(bf16[448,64]{1,0:T(8,128)(2,1)} %copy-done.35) | copy-start | bytes 172036
  158.9 17.9 %copy-start.38 = (bf16[448,64]{1,0:T(8,128)(2,1)S(1)}, bf16[448,64]{1,0:T(8,128)(2,1)}, u32[]{:S(2)}) copy-start(bf16[448,64]{1,0:T(8,128)(2,1)} %copy-done.37) | copy-start | bytes 172036
  178.9 10.3 %copy-start.22 = (bf16[256,448]{0,1:T(8,128)(2,1)S(1)}, bf16[256,448]{0,1:T(8,128)(2,1)}, u32[]{:S(2)}) copy-start(bf16[256,448]{0,1:T(8,128)(2,1)} %copy-done.21) | copy-start | bytes 688132
  178.9 92.1 %reduce-scatter.24.cloned.1.call-start = ((), (), s32[]{:S(2)}) async-start(), calls=%async_computation.17 | async-start | bytes 688128 | tf_op jit(solution)/shard_map/reduce_scatter | solution.py:114
  189.1 1.7 copy-start.4
  189.2 115.1 %all-reduce.5.cloned.1.call-start = ((), (), s32[]{:S(2)}) async-start(), calls=%async_computation.28 | async-start | bytes 2293760
  190.6 271.1 %reduce-scatter.36.cloned.1.call-start = ((), (), s32[]{:S(2)}) async-start(), calls=%async_computation.24 | async-start | bytes 9805824 | tf_op jit(solution)/shard_map/reduce_scatter | solution.py:93
  197.3 1.0 copy-start.14
  197.3 2.4 copy-start.16
  197.3 330.6 %reduce-scatter.34.cloned.1.call-start = ((), (), s32[]{:S(2)}) async-start(), calls=%async_computation.23 | async-start | bytes 1032192 | tf_op jit(solution)/shard_map/reduce_scatter | solution.py:93
  199.6 430.5 %reduce-scatter.38.cloned.1.call-start = ((), (), s32[]{:S(2)}) async-start(), calls=%async_computation.25 | async-start | bytes 5603328 | tf_op jit(solution)/shard_map/reduce_scatter | solution.py:93
  204.1 24.3 %copy-start.42 = (f32[448]{0:T(512)S(1)}, f32[448]{0:T(512)}, u32[]{:S(2)}) copy-start(f32[448]{0:T(512)} %param.18) | copy-start | bytes 5380
  204.1 24.3 %copy-start.49 = (f32[128]{0:T(128)S(1)}, f32[128]{0:T(128)}, u32[]{:S(2)}) copy-start(f32[128]{0:T(128)} %copy-done.48) | copy-start | bytes 1540
  204.1 28.0 %copy-start.45 = (f32[448]{0:T(512)S(1)}, f32[448]{0:T(512)}, u32[]{:S(2)}) copy-start(f32[448]{0:T(512)} %get-tuple-element.14) | copy-start | bytes 5380
  204.2 66.8 %copy-start.57 = (f32[128]{0:T(128)S(1)}, f32[128]{0:T(128)}, u32[]{:S(2)}) copy-start(f32[128]{0:T(128)} %copy-done.56) | copy-start | bytes 1540
  204.2 66.8 %copy-start.8 = (f32[128,448]{0,1:T(8,128)S(1)}, f32[128,448]{0,1:T(8,128)}, u32[]{:S(2)}) copy-start(f32[128,448]{0,1:T(8,128)} %reduce-scatter.28.cloned.1.call-done) | copy-start | bytes 688132
  204.2 66.8 %copy-start.20 = (bf16[128,448]{0,1:T(8,128)(2,1)S(1)}, bf16[128,448]{0,1:T(8,128)(2,1)}, u32[]{:S(2)}) copy-start(bf16[128,448]{0,1:T(8,128)(2,1)} %param.17) | copy-start | bytes 344068
  204.2 66.8 %copy-start.41 = (f32[448]{0:T(512)S(1)}, f32[448]{0:T(512)}, u32[]{:S(2)}) copy-start(f32[448]{0:T(512)} %param.26) | copy-start | bytes 5380
  204.2 66.8 %copy-start.47 = (f32[128]{0:T(128)S(1)}, f32[128]{0:T(128)}, u32[]{:S(2)}) copy-start(f32[128]{0:T(128)} %copy-done.46) | copy-start | bytes 1540
  204.2 66.8 %copy-start.52 = (f32[128]{0:T(128)S(1)}, f32[128]{0:T(128)}, u32[]{:S(2)}) copy-start(f32[128]{0:T(128)} %copy-done.51) | copy-start | bytes 1540
  (11 other events, 7.5 us)
Sparse Core Ops, SparseCore 0:
  23.7 9.5 reduce-scatter.17
  43.0 14.9 reduce-scatter.19
  60.3 10.0 reduce-scatter.25
  77.3 13.0 reduce-scatter.21
  95.2 12.3 all-gather.6
  112.9 14.9 reduce-scatter.27
  142.4 7.8 reduce-scatter.29
  153.7 8.5 reduce-scatter.41
  165.1 8.6 reduce-scatter.39
  175.8 10.4 all-gather.4
  189.1 14.9 reduce-scatter.31
  206.9 13.8 reduce-scatter.23
  224.3 79.9 all-reduce.4
  308.2 153.4 reduce-scatter.35
  465.9 61.9 reduce-scatter.33
  532.0 98.0 reduce-scatter.37
where the time goes:
time: 638 us; the launch traced here: 637 us
  waiting for transfers between devices  432 us (68%)
  blocking collectives  105 us (16%)
  matrix products  40.1 us (6%)
  local copies, waits for them, and re-layouts  22 us (3%)
  other arithmetic  21.2 us (3%)
  between operations  15.4 us (2%)
    reduce_scatter x3, waiting for transfers between devices, data_total(): lax.psum_scatter(outer_sum(left_side, right_side), 'dp', scatter_dimensio...  320 us
    unnamed x19, waiting for transfers between devices  46.1 us
    psum x1, blocking collectives, per_device(): gain1_final, gain2_final = lax.psum((gain1_part, gain2_part), ('dp', 'row'))  38.9 us
    reduce_scatter x4, waiting for transfers between devices, across_columns(): lax.psum_scatter(partial_term(jnp.int32(0), lax.axis_size('col') * row_co...  29.7 us
    all_gather x4, blocking collectives, spread_rows(): return lax.all_gather(values, 'row', axis=0, tiled=True)  24.9 us
    psum x1, blocking collectives, per_device(): lax.psum((bias_part[:query_width], bias_part[query_width:query_width + ke...  22.2 us
    all_gather x2, waiting for transfers between devices, spread_cols(): return lax.all_gather(values, 'col', axis=0, tiled=True)  19.8 us
    reduce_scatter x4, waiting for transfers between devices, across_rows(): lax.psum_scatter(partial_term(jnp.int32(0), lax.axis_size('row') * row_co...  16.2 us
  transfers between devices with their start and end apart: 16, of which 13 were waited for; matrix products, arithmetic and copies ran while one was open for 8% of the time, Pallas kernels for 0%

commit v1 on v0

--- a/solution.py
+++ b/solution.py
@@ -1,10 +1,15 @@
+import functools
+
 import jax
 import jax.numpy as jnp
 from jax import lax
+from jax.experimental import pallas as pl
+from jax.experimental.pallas import tpu as pltpu
 from jax.sharding import PartitionSpec as P
 
 D = 896
 HD = 64
+MESH = pl.DeviceIdType.MESH
 
 
 NEGATIVE = -1e30
@@ -83,16 +88,6 @@
     return jnp.dot(left_side, weight, preferred_element_type=jnp.float32)
 
 
-def outer_sum(left_side, right_side):
-    return lax.dot_general(
-        left_side, right_side, (((0,), (0,)), ((), ())), preferred_element_type=jnp.float32
-    )
-
-
-def data_total(left_side, right_side):
-    return lax.psum_scatter(outer_sum(left_side, right_side), "dp", scatter_dimension=0, tiled=True)
-
-
 def across_columns(gathered, weight, flipped, row_count):
 
     def partial_term(first_row, how_many):
@@ -117,6 +112,256 @@
         scatter_dimension=0,
         tiled=True,
     )
+
+
+def line_kernel(
+    line,
+    lhs_second,
+    rhs_both,
+    lhs_down,
+    rhs_down,
+    lhs_mixed,
+    rhs_branch,
+    lhs_first,
+    rhs_projected,
+    small_part,
+    gate_up_out,
+    down_out,
+    joint_out,
+    small_out,
+    *scratch,
+):
+    send, below, above = scratch[0:3], scratch[3:6], scratch[6:9]
+    small_send, small_below, small_above = scratch[9:12]
+    send_sem, below_sem, above_sem, small_sem = scratch[12:16]
+    index = lax.axis_index("dp")
+    place = index // 2
+    has_below = place > 0
+    has_above = place < line - 1
+    lower = {"dp": lax.rem(index + 2 * line - 2, 2 * line)}
+    upper = {"dp": lax.rem(index + 2, 2 * line)}
+    hidden_width = rhs_both.shape[1] // 2
+
+    barrier = pltpu.get_barrier_semaphore()
+
+    @pl.when(has_below)
+    def _():
+        pl.semaphore_signal(barrier, inc=1, device_id=lower, device_id_type=MESH)
+
+    @pl.when(has_above)
+    def _():
+        pl.semaphore_signal(barrier, inc=1, device_id=upper, device_id_type=MESH)
+
+    pl.semaphore_wait(barrier, has_below.astype(jnp.int32) + has_above.astype(jnp.int32))
+
+    def term(piece, target):
+        def dot(left, right):
+            return jnp.dot(left, right, preferred_element_type=jnp.float32)
+
+        if piece == 0:
+            left = lhs_second[target]
+            return jnp.concatenate(
+                [dot(left, rhs_both[:, :hidden_width]), dot(left, rhs_both[:, hidden_width:])], 0
+            )
+        if piece == 1:
+            return dot(lhs_down[target], rhs_down[...])
+        return jnp.concatenate(
+            [dot(lhs_mixed[target], rhs_branch[...]), dot(lhs_first[target], rhs_projected[...])], 0
+        )
+
+    outs = (gate_up_out, down_out, joint_out)
+
+    def copy_up(piece, target):
+        return pltpu.make_async_remote_copy(
+            src_ref=send[piece].at[target],
+            dst_ref=below[piece].at[target],
+            send_sem=send_sem.at[piece, target],
+            recv_sem=below_sem.at[piece, target],
+            device_id=upper,
+            device_id_type=MESH,
+        )
+
+    def copy_down(piece, target):
+        return pltpu.make_async_remote_copy(
+            src_ref=send[piece].at[target],
+            dst_ref=above[piece].at[target],
+            send_sem=send_sem.at[piece, target],
+            recv_sem=above_sem.at[piece, target],
+            device_id=lower,
+            device_id_type=MESH,
+        )
+
+    def small_copy(source, landing, at, device):
+        return pltpu.make_async_remote_copy(
+            src_ref=source,
+            dst_ref=landing,
+            send_sem=small_sem.at[at],
+            recv_sem=small_sem.at[at + 1],
+            device_id=device,
+            device_id_type=MESH,
+        )
+
+    small_up = small_copy(small_send.at[0], small_below, 0, upper)
+    small_down = small_copy(small_send.at[1], small_above, 2, lower)
+
+    @pl.when(jnp.logical_not(has_below))
+    def _():
+        small_below[...] = jnp.zeros_like(small_below)
+
+    @pl.when(has_below)
+    def _():
+        small_up.wait_recv()
+
+    @pl.when(has_above)
+    def _():
+        small_send[0] = small_below[...] + small_part[...]
+        small_up.start()
+
+    @pl.when(jnp.logical_not(has_above))
+    def _():
+        small_above[...] = jnp.zeros_like(small_above)
+
+    def step(count, carry):
+        half = count // 2
+        target = jnp.where(count % 2 == 0, line - 1 - half, half)
+        for piece in range(3):
+
+            @pl.when(target > place)
+            def _():
+                own = term(piece, target)
+
+                @pl.when(has_below)
+                def _():
+                    copy_up(piece, target).wait_recv()
+                    send[piece][target] = (own + below[piece][target].astype(jnp.float32)).astype(
+                        jnp.bfloat16
+                    )
+
+                @pl.when(jnp.logical_not(has_below))
+                def _():
+                    send[piece][target] = own.astype(jnp.bfloat16)
+
+                copy_up(piece, target).start()
+
+            @pl.when(target < place)
+            def _():
+                own = term(piece, target)
+
+                @pl.when(has_above)
+                def _():
+                    copy_down(piece, target).wait_recv()
+                    send[piece][target] = (own + above[piece][target].astype(jnp.float32)).astype(
+                        jnp.bfloat16
+                    )
+
+                @pl.when(jnp.logical_not(has_above))
+                def _():
+                    send[piece][target] = own.astype(jnp.bfloat16)
+
+                copy_down(piece, target).start()
+
+            @pl.when(target == place)
+            def _():
+                outs[piece][...] = term(piece, target)
+
+        return carry
+
+    lax.fori_loop(0, line, step, 0)
+
+    @pl.when(has_above)
+    def _():
+        small_down.wait_recv()
+
+    @pl.when(has_below)
+    def _():
+        small_send[1] = small_above[...] + small_part[...]
+        small_down.start()
+
+    small_out[...] = small_below[...] + small_part[...] + small_above[...]
+
+    for piece in range(3):
+
+        @pl.when(has_below)
+        def _():
+            copy_up(piece, place).wait_recv()
+            outs[piece][...] += below[piece][place].astype(jnp.float32)
+
+        @pl.when(has_above)
+        def _():
+            copy_down(piece, place).wait_recv()
+            outs[piece][...] += above[piece][place].astype(jnp.float32)
+
+    def finish(target, carry):
+        for piece in range(3):
+
+            @pl.when(target != place)
+            def _():
+                copy_up(piece, target).wait_send()
+
+        return carry
+
+    lax.fori_loop(0, line, finish, 0)
+
+    @pl.when(has_above)
+    def _():
+        small_up.wait_send()
+
+    @pl.when(has_below)
+    def _():
+        small_down.wait_send()
+
+
+def line_totals(line, operands):
+    lhs_second, rhs_both, lhs_down, rhs_down, lhs_mixed, rhs_branch, _, rhs_projected, small = (
+        operands
+    )
+    shapes = (
+        (2 * lhs_second.shape[1], rhs_both.shape[1] // 2),
+        (lhs_down.shape[1], rhs_down.shape[1]),
+        (2 * lhs_mixed.shape[1], rhs_projected.shape[1]),
+    )
+    slots = [pltpu.VMEM((line,) + shape, jnp.bfloat16) for shape in shapes]
+    vmem = pl.BlockSpec(memory_space=pltpu.VMEM)
+    return pl.pallas_call(
+        functools.partial(line_kernel, line),
+        out_shape=[jax.ShapeDtypeStruct(shape, jnp.float32) for shape in shapes]
+        + [jax.ShapeDtypeStruct(small.shape, jnp.float32)],
+        in_specs=[vmem] * 9,
+        out_specs=[vmem] * 4,
+        scratch_shapes=slots * 3
+        + [
+            pltpu.VMEM((2,) + small.shape, jnp.float32),
+            pltpu.VMEM(small.shape, jnp.float32),
+            pltpu.VMEM(small.shape, jnp.float32),
+            pltpu.SemaphoreType.DMA((3, line)),
+            pltpu.SemaphoreType.DMA((3, line)),
+            pltpu.SemaphoreType.DMA((3, line)),
+            pltpu.SemaphoreType.DMA((4,)),
+        ],
+        compiler_params=pltpu.CompilerParams(
+            collective_id=0, has_side_effects=True, vmem_limit_bytes=56 * 1024 * 1024
+        ),
+    )(*operands)
+
+
+def swap_pair(values):
+    count = lax.axis_size("dp")
+    return lax.ppermute(values, "dp", [(i, i ^ 1) for i in range(count)])
+
+
+def pair_left(gathered):
+    line = lax.axis_size("dp") // 2
+    rows, columns = gathered.shape
+    blocks = gathered.T.reshape(line, 2, columns // (2 * line), rows)
+    mine = lax.axis_index("dp") % 2
+    theirs = lax.dynamic_index_in_dim(blocks, 1 - mine, 1, keepdims=False)
+    return jnp.concatenate(
+        [lax.dynamic_index_in_dim(blocks, mine, 1, keepdims=False), swap_pair(theirs)], -1
+    )
+
+
+def pair_right(gathered):
+    return jnp.concatenate([gathered, swap_pair(gathered)], 0)
 
 
 def per_device(
@@ -262,24 +507,45 @@
     grad_normed1 = across_rows(grad_projected_all, joint_weight, True, local_rows)
     back_first, gain1_part = norm_backward(grad_normed1, inputs, inverse1, norm1_gain)
     input_grad = (grad_hidden + back_first).astype(jnp.bfloat16)
-    gain1_final, gain2_final = lax.psum((gain1_part, gain2_part), ("dp", "row"))
-    qbias_final, kbias_final, vbias_final = lax.psum(
+    def row_pair(values):
+        size = lax.axis_size("row")
+        return values + lax.ppermute(values, "row", [(i, (i + 1) % size) for i in range(size)])
+
+    line = lax.axis_size("dp") // 2
+    feature_width = inputs.shape[1]
+    gains = row_pair(jnp.concatenate([gain1_part, gain2_part]))
+    small = jnp.concatenate([gains, bias_part])
+    small = small + swap_pair(small)
+    small_length = small.shape[0]
+    small = jnp.pad(small, (0, -small_length % 1024)).reshape(-1, 128)
+    rhs_both = jnp.concatenate([grad_both_all, spread_cols(swap_pair(grad_both))], 0)
+    padding = ((0, 0), (0, 2 * key_width))
+    gate_up_total, down_final, joint_total, small_total = line_totals(
+        line,
         (
-            bias_part[:query_width],
-            bias_part[query_width : query_width + key_width],
-            bias_part[query_width + key_width :],
+            pair_left(normed2_all),
+            rhs_both,
+            pair_left(activated_all),
+            pair_right(grad_output_all),
+            pair_left(mixed_all),
+            jnp.pad(pair_right(grad_branch_all), padding),
+            pair_left(normed1_all),
+            pair_right(grad_projected_all),
+            small,
         ),
-        "dp",
-    )
-    down_final = data_total(activated_all, grad_output_all)
-    gate_up_final = data_total(normed2_all, grad_both_all)
-    output_final = data_total(mixed_all, grad_branch_all)
-    joint_final = data_total(normed1_all, grad_projected_all)
+    )
+    block = feature_width // (2 * line)
+    gate_final, up_final = gate_up_total[:block], gate_up_total[block:]
+    output_final, joint_final = joint_total[:block, :query_width], joint_total[block:]
     query_final = joint_final[:, :query_width]
     key_final = joint_final[:, query_width : query_width + key_width]
     value_final = joint_final[:, query_width + key_width :]
-    gate_final = gate_up_final[:, :hidden_width]
-    up_final = gate_up_final[:, hidden_width:]
+    small_flat = small_total.reshape(-1)
+    cuts = [feature_width, feature_width, query_width, key_width, key_width]
+    ends = [sum(cuts[: i + 1]) for i in range(len(cuts))]
+    gain1_final, gain2_final, qbias_final, kbias_final, vbias_final = (
+        small_flat[end - cut : end] for end, cut in zip(ends, cuts)
+    )
     return (
         output,
         input_grad,

time: 638 us -> 380 us (0.60)
  waiting for transfers between devices: 432 us -> 114 us
  Pallas kernels: 0 us -> 93.6 us
  blocking collectives: 105 us -> 44.9 us
  other arithmetic: 21.2 us -> 35.9 us
  local copies, waits for them, and re-layouts: 22 us -> 36.3 us
  matrix products: 40.1 us -> 27.7 us
  starting transfers between devices: 0.84 us -> 11.3 us
    reduce_scatter x3 -> x2, waiting for transfers between devices: 320 us -> 0.04 us  [the longest x1 0.02 us: per_device(): lax.psum_scatter(grad_values_part.astype(jnp.bfloat16), 'col', scatter_di...]
    pallas_call x0 -> x1, Pallas kernels: none -> 93.6 us  [line_totals(): pl.pallas_call(functools.partial(line_kernel, line), out_shape=[jax.Shape...]
    psum x2 -> x0, blocking collectives: 61 us -> none  [the longest x1 38.9 us: per_device(): gain1_final, gain2_final = lax.psum((gain1_part, gain2_part), ('dp', 'row'))]
    ppermute x0 -> x10, waiting for transfers between devices: none -> 55.9 us  [the longest x9 55.9 us: swap_pair(): return lax.ppermute(values, 'dp', [(i, i ^ 1) for i in range(count)])]
    unnamed x19 -> x13, waiting for transfers between devices: 46.1 us -> 0.21 us
    concatenate x0 -> x10, other arithmetic: none -> 15.1 us  [the longest x4 5.31 us: pair_left(): jnp.concatenate([lax.dynamic_index_in_dim(blocks, mine, 1, keepdims=False...]
    dot_general x4 -> x0, matrix products: 13.5 us -> none  [outer_sum(): lax.dot_general(left_side, right_side, (((0,), (0,)), ((), ())), preferre...]
    ppermute x0 -> x10, starting transfers between devices: none -> 10.6 us  [the longest x9 9.12 us: swap_pair(): return lax.ppermute(values, 'dp', [(i, i ^ 1) for i in range(count)])]
  transfers between devices with their start and end apart: 16 -> 23, of which waited for: 13 -> 13; matrix products, arithmetic and copies ran while one was open for 8% -> 14% of each run, Pallas kernels for 0% -> 0%
where the time goes in v1:
time: 380 us; the launch traced here: 379 us
  waiting for transfers between devices  114 us (30%)
  Pallas kernels  93.6 us (25%)
  blocking collectives  44.9 us (12%)
  local copies, waits for them, and re-layouts  36.3 us (10%)
  other arithmetic  35.9 us (9%)
  matrix products  27.7 us (7%)
  between operations  14.7 us (4%)
  starting transfers between devices  11.3 us (3%)
    pallas_call x1, Pallas kernels, line_totals(): pl.pallas_call(functools.partial(line_kernel, line), out_shape=[jax.Shape...  93.6 us
    ppermute x9, waiting for transfers between devices, swap_pair(): return lax.ppermute(values, 'dp', [(i, i ^ 1) for i in range(count)])  55.9 us
    reduce_scatter x4, waiting for transfers between devices, across_columns(): lax.psum_scatter(partial_term(jnp.int32(0), lax.axis_size('col') * row_co...  29.6 us
    all_gather x4, blocking collectives, spread_rows(): return lax.all_gather(values, 'row', axis=0, tiled=True)  26.8 us
    reduce_scatter x4, waiting for transfers between devices, across_rows(): lax.psum_scatter(partial_term(jnp.int32(0), lax.axis_size('row') * row_co...  16.2 us
    unnamed x116, local copies, waits for them, and re-layouts  13.1 us
    all_gather x3, waiting for transfers between devices, spread_cols(): return lax.all_gather(values, 'col', axis=0, tiled=True)  12.5 us
    dot_general x4, matrix products, product(): lax.dot_general(left_side, weight, (((1,), (1,)), ((), ())), preferred_el...  11.9 us
  transfers between devices with their start and end apart: 23, of which 13 were waited for; matrix products, arithmetic and copies ran while one was open for 14% of the time, Pallas kernels for 0%

profile of v1, /device:TPU:0, one launch (start us, length us, event | category | flops | bytes accessed | tf_op | source)
XLA Modules:
  0.0 378.7 jit_solution(1069856109956026820)
XLA Ops:
  7.3 1.2 copy.135
  8.6 2.6 psum.28
  12.5 7.3 %all_gather.33 = bf16[256,448]{1,0:T(8,128)(2,1)S(1)} all-gather(bf16[128,448]{1,0:T(8,128)(2,1)S(1)} %fusion.20), channel_id=1, replica_groups=mesh['dp'=8,'row'=2,'col'=2] {'row'}, dimensions={0}, use_global_device_ids=true | all-gather | bytes 344064 | tf_op jit(solution)/shard_map/all_gather | solution.py:76
  21.9 1.3 fusion.28
  25.1 7.9 %reduce-scatter.11.cloned.1.call-done = f32[128,576]{1,0:T(8,128)} async-done(((f32[256,576]{1,0:T(8,128)}), f32[128,576]{1,0:T(8,128)}) %reduce-scatter.11.cloned.1.call-update) | async-done | bytes 294928 | tf_op jit(solution)/shard_map/reduce_scatter | solution.py:96
  36.8 1.8 copy.140
  40.3 2.1 all-gather.1
  42.4 2.1 all-gather
  44.5 1.2 fusion.58
  46.1 2.0 all_gather.36
  48.1 1.1 fusion.59
  49.3 1.7 copy.150
  51.0 6.6 %all_gather.39 = bf16[256,448]{1,0:T(8,128)(2,1)S(1)} all-gather(bf16[128,448]{1,0:T(8,128)(2,1)} %copy.150), channel_id=1, replica_groups=mesh['dp'=8,'row'=2,'col'=2] {'row'}, dimensions={0}, use_global_device_ids=true | all-gather | bytes 344064 | tf_op jit(solution)/shard_map/all_gather | solution.py:76
  57.6 2.3 fusion.62
  59.9 3.3 constant_dynamic-update-slice_fusion.1
  63.2 1.6 constant_dynamic-update-slice_fusion
  65.1 1.1 multiply_reduce_fusion.3
  66.2 2.5 psum.29
  68.8 6.5 %all_gather.37 = bf16[256,448]{1,0:T(8,128)(2,1)S(1)} all-gather(bf16[128,448]{1,0:T(8,128)(2,1)S(1)} %multiply_convert_fusion.4), channel_id=1, replica_groups=mesh['dp'=8,'row'=2,'col'=2] {'row'}, dimensions={0}, use_global_device_ids=true | all-gather | bytes 344064 | tf_op jit(solution)/shard_map/all_gather | solution.py:76
  76.0 6.2 %fusion.60 = f32[256,4864]{1,0:T(8,128)} fusion(bf16[256,448]{1,0:T(8,128)(2,1)S(1)} %all_gather.37, bf16[448,4864]{1,0:T(8,128)(2,1)} %constant_dynamic-update-slice_fusion), kind=kOutput, calls=%fused_computation.148 | convolution fusion | flops 1115684864 | bytes 9568256 | tf_op jit(solution)/shard_map/dot_general | solution.py:88
  82.3 13.7 %reduce-scatter.15.cloned.1.call-done = f32[128,4864]{1,0:T(8,128)} async-done(((f32[256,4864]{1,0:T(8,128)}), f32[128,4864]{1,0:T(8,128)}) %reduce-scatter.15.cloned.1.call-update) | async-done | bytes 2490384 | tf_op jit(solution)/shard_map/reduce_scatter | solution.py:96
  96.0 3.5 multiply_convert_fusion.1
  99.6 1.1 pad_maximum_fusion.1
  100.8 12.5 %all-gather.8.cloned.1.call-done = bf16[256,4864]{1,0:T(8,128)(2,1)} async-done(((bf16[128,4864]{1,0:T(8,128)(2,1)}), bf16[256,4864]{1,0:T(8,128)(2,1)}) %all-gather.8.cloned.1.call-update) | async-done | bytes 2490384 | tf_op jit(solution)/shard_map/all_gather | solution.py:80
  113.3 5.3 %fusion.63 = f32[256,448]{1,0:T(8,128)} fusion(bf16[256,4864]{1,0:T(8,128)(2,1)} %all-gather.8.cloned.1.call-done, bf16[448,4864]{1,0:T(8,128)(2,1)} %constant_dynamic-update-slice_fusion), kind=kOutput, calls=%fused_computation.151 | convolution fusion | flops 1115684864 | bytes 7307264 | tf_op jit(solution)/shard_map/dot_general | solution.py:85
  118.6 15.8 %reduce-scatter.21.cloned.1.call-done = f32[128,448]{1,0:T(8,128)} async-done(((f32[256,448]{1,0:T(8,128)}), f32[128,448]{1,0:T(8,128)}) %reduce-scatter.21.cloned.1.call-update) | async-done | bytes 229392 | tf_op jit(solution)/shard_map/reduce_scatter | solution.py:109
  134.4 1.7 multiply_reduce_fusion.1
  136.1 2.4 psum.30
  138.6 1.1 fusion.50
  139.7 6.4 %all_gather.41 = bf16[256,448]{1,0:T(8,128)(2,1)} all-gather(bf16[128,448]{1,0:T(8,128)(2,1)S(1)} %fusion.50), channel_id=1, replica_groups=mesh['dp'=8,'row'=2,'col'=2] {'row'}, dimensions={0}, use_global_device_ids=true | all-gather | bytes 344064 | tf_op jit(solution)/shard_map/all_gather | solution.py:76
  146.1 2.0 fusion.64
  148.2 7.9 %reduce-scatter.23.cloned.1.call-done = f32[128,448]{0,1:T(8,128)} async-done(((f32[256,448]{0,1:T(8,128)}), f32[128,448]{0,1:T(8,128)}) %reduce-scatter.23.cloned.1.call-update) | async-done | bytes 229392 | tf_op jit(solution)/shard_map/reduce_scatter | solution.py:96
  157.1 1.2 multiply_reduce_fusion
  160.3 1.8 fusion.9
  162.2 1.8 collective-permute-start.1
  164.0 28.1 %collective-permute-done.1 = bf16[128,4864]{1,0:T(8,128)(2,1)} collective-permute-done((bf16[128,4864]{1,0:T(8,128)(2,1)}, bf16[128,4864]{1,0:T(8,128)(2,1)}, u32[]{:S(2)}, u32[]{:S(2)}) %collective-permute-start.1) | collective-permute-done | bytes 1245216 | tf_op jit(solution)/shard_map/ppermute | solution.py:349
  194.1 1.8 collective-permute-start.6
  196.2 4.0 %collective-permute-done.6 = bf16[4,56,256]{2,1,0:T(8,128)(2,1)S(1)} collective-permute-done((bf16[4,56,256]{2,1,0:T(8,128)(2,1)S(1)}, bf16[4,56,256]{2,1,0:T(8,128)(2,1)S(1)}, u32[]{:S(2)}, u32[]{:S(2)}) %collective-permute-start.6) | collective-permute-done | bytes 114720 | tf_op jit(solution)/shard_map/ppermute | solution.py:349
  200.8 3.7 collective-permute-done.3
  209.4 2.0 all_gather.42
  211.5 2.3 fusion.27
  214.8 1.5 collective-permute-start.4
  217.1 2.4 copy.164
  219.6 2.2 dynamic-slice_bitcast_fusion.1
  222.3 1.6 collective-permute-start
  223.9 1.6 pad_maximum_fusion.8.lhs_mixed
  225.5 14.7 %collective-permute-done = bf16[4,56,256]{2,1,0:T(8,128)(2,1)S(1)} collective-permute-done((bf16[4,56,256]{2,1,0:T(8,128)(2,1)S(1)}, bf16[4,56,256]{2,1,0:T(8,128)(2,1)S(1)}, u32[]{:S(2)}, u32[]{:S(2)}) %collective-permute-start) | collective-permute-done | bytes 114720 | tf_op jit(solution)/shard_map/ppermute | solution.py:349
  241.5 1.7 fusion.61
  243.2 2.3 pad_maximum_fusion.2.lhs_down
  245.5 3.0 collective-permute-done.5
  248.5 2.0 fusion.12.rhs_branch
  251.0 5.0 %pad_maximum_fusion.rhs_both = bf16[512,4864]{1,0:T(8,128)(2,1)} fusion(bf16[256,4864]{1,0:T(8,128)(2,1)} %all-gather.10.cloned.1.call-done, bf16[256,4864]{1,0:T(8,128)(2,1)} %all-gather.8.cloned.1.call-done), kind=kLoop, calls=%fused_computation | loop fusion | flops 9961472 | bytes 9961472 | tf_op jit(solution)/shard_map/concatenate | solution.py:521
  256.1 2.1 collective-permute-done.7
  258.2 1.9 pad_maximum_fusion.3.rhs_projected
  260.1 1.1 fusion.26
  261.3 1.5 collective-permute-start.8
  262.8 2.4 psum.31
  266.0 1.2 fusion.24
  269.6 93.6 %shard_map.254 = (f32[112,2432]{1,0:T(8,128)}, f32[304,448]{1,0:T(8,128)}, f32[112,576]{1,0:T(8,128)}, f32[16,128]{1,0:T(8,128)}) custom-call(bf16[4,56,512]{2,1,0:T(8,128)(2,1)} %pad_maximum_fusion.7.lhs_second, bf16[512,4864]{1,0:T(8,128)(2,1)} %pad_maximum_fusion.rhs_both, bf16[4,304,512]{2,1,0:T(8,128)(2,1)} %pad_maximum_fusion.2.lhs_down, ...), custom_call_target="tpu_custom_call" | custom-call | tf_op jit(solution)/shard_map/pallas_call | solution.py:325
  363.2 1.7 fusion.52
  364.9 1.5 fusion.53
  366.4 1.4 fusion.56
  367.8 1.3 fusion.57
  369.1 2.3 fusion.51
  (222 shorter events, 31.7 us)
Async XLA Ops:
  7.2 50.4 %copy-start = (bf16[2432,448]{0,1:T(8,128)(2,1)S(1)}, bf16[2432,448]{0,1:T(8,128)(2,1)}, u32[]{:S(2)}) copy-start(bf16[2432,448]{0,1:T(8,128)(2,1)} %param.29) | copy-start | bytes 6537220
  7.2 14.7 %copy-start.50 = (bf16[448,448]{1,0:T(8,128)(2,1)S(1)}, bf16[448,448]{1,0:T(8,128)(2,1)}, u32[]{:S(2)}) copy-start(bf16[448,448]{1,0:T(8,128)(2,1)} %param.19) | copy-start | bytes 1204228
  7.2 25.8 %reduce-scatter.11.cloned.1.call-start = ((), (), s32[]{:S(2)}) async-start(), calls=%async_computation.10 | async-start | bytes 983040 | tf_op jit(solution)/shard_map/reduce_scatter | solution.py:96
  19.8 3.4 copy-start.19
  20.8 2.4 copy-start.34
  21.9 2.0 copy-start.47
  21.9 2.0 copy-start.48
  23.3 41.9 %reduce-scatter.13.cloned.1.call-start = ((), (), s32[]{:S(2)}) async-start(), calls=%async_computation.11 | async-start | bytes 786432 | tf_op jit(solution)/shard_map/reduce_scatter | solution.py:109
  25.0 10.5 %copy-start.26 = (f32[128,32]{1,0:T(8,128)}, f32[128,32]{1,0:T(8,128)S(1)}, u32[]{:S(2)}) copy-start(f32[128,32]{1,0:T(8,128)S(1)} %get-tuple-element.120) | copy-start | bytes 49156
  25.1 10.5 %copy-start.27 = (f32[128,32]{1,0:T(8,128)}, f32[128,32]{1,0:T(8,128)S(1)}, u32[]{:S(2)}) copy-start(f32[128,32]{1,0:T(8,128)S(1)} %get-tuple-element.119) | copy-start | bytes 49156
  35.6 2.9 copy-start.31
  35.8 3.8 copy-start.12
  35.8 8.6 %copy-start.14 = (f32[128,7,64]{0,2,1:T(8,128)}, f32[128,7,64]{0,2,1:T(8,128)S(1)}, u32[]{:S(2)}) copy-start(f32[128,7,64]{0,2,1:T(8,128)S(1)} %maximum_multiply_fusion) | copy-start | bytes 688132
  36.1 122.4 %copy-start.28 = (f32[128,64]{0,1:T(8,128)}, f32[128,64]{0,1:T(8,128)S(1)}, u32[]{:S(2)}) copy-start(f32[128,64]{0,1:T(8,128)S(1)} %copy.139) | copy-start | bytes 98308
  42.4 3.7 copy-start.24
  45.8 2.3 copy-start.16
  49.2 33.1 %reduce-scatter.19.cloned.1.call-start = ((), (), s32[]{:S(2)}) async-start(), calls=%async_computation.15 | async-start | bytes 3735552 | tf_op jit(solution)/shard_map/reduce_scatter | solution.py:96
  57.6 2.3 copy-start.5
  59.9 36.2 %reduce-scatter.15.cloned.1.call-start = ((), (), s32[]{:S(2)}) async-start(), calls=%async_computation.12 | async-start | bytes 7471104 | tf_op jit(solution)/shard_map/reduce_scatter | solution.py:96
  59.9 3.3 copy-start.8
  63.2 5.5 %copy-start.37 = (f32[448]{0:T(512)S(1)}, f32[448]{0:T(512)}, u32[]{:S(2)}) copy-start(f32[448]{0:T(512)} %param.26) | copy-start | bytes 5380
  68.7 69.9 %copy-start.41 = (f32[128]{0:T(128)}, f32[128]{0:T(128)S(1)}, u32[]{:S(2)}) copy-start(f32[128]{0:T(128)S(1)} %add_rsqrt_fusion) | copy-start | bytes 1540
  82.2 31.0 %all-gather.8.cloned.1.call-start = ((), (), s32[]{:S(2)}) async-start(), calls=%async_computation.16 | async-start | bytes 3735552 | tf_op jit(solution)/shard_map/all_gather | solution.py:80
  100.7 33.7 %reduce-scatter.21.cloned.1.call-start = ((), (), s32[]{:S(2)}) async-start(), calls=%async_computation.17 | async-start | bytes 786432 | tf_op jit(solution)/shard_map/reduce_scatter | solution.py:109
  118.5 37.6 %reduce-scatter.23.cloned.1.call-start = ((), (), s32[]{:S(2)}) async-start(), calls=%async_computation.18 | async-start | bytes 688128 | tf_op jit(solution)/shard_map/reduce_scatter | solution.py:96
  138.5 7.5 %copy-start.17 = (bf16[448,448]{1,0:T(8,128)(2,1)S(1)}, bf16[448,448]{1,0:T(8,128)(2,1)}, u32[]{:S(2)}) copy-start(bf16[448,448]{1,0:T(8,128)(2,1)} %param.25) | copy-start | bytes 1204228
  138.6 9.6 %copy-start.45 = (f32[128]{0:T(128)}, f32[128]{0:T(128)S(1)}, u32[]{:S(2)}) copy-start(f32[128]{0:T(128)S(1)} %fusion.45) | copy-start | bytes 1540
  148.1 58.3 %reduce-scatter.25.cloned.1.call-start = ((), (), s32[]{:S(2)}) async-start(), calls=%async_computation.19 | async-start | bytes 98304 | tf_op jit(solution)/shard_map/reduce_scatter | solution.py:492
  160.2 48.3 %reduce-scatter.27.cloned.1.call-start = ((), (), s32[]{:S(2)}) async-start(), calls=%async_computation.20 | async-start | bytes 98304 | tf_op jit(solution)/shard_map/reduce_scatter | solution.py:495
  162.1 30.1 %copy-start.20 = (bf16[256,448]{1,0:T(8,128)(2,1)S(1)}, bf16[256,448]{1,0:T(8,128)(2,1)}, u32[]{:S(2)}) copy-start(bf16[256,448]{1,0:T(8,128)(2,1)} %copy-done.19) | copy-start | bytes 688132
  162.1 55.0 %all-gather.6.cloned.1.call-start = ((), (), s32[]{:S(2)}) async-start(), calls=%async_computation.13 | async-start | bytes 1867776 | tf_op jit(solution)/shard_map/all_gather | solution.py:80
  162.2 30.0 %collective-permute-start.1 = (bf16[128,4864]{1,0:T(8,128)(2,1)}, bf16[128,4864]{1,0:T(8,128)(2,1)}, u32[]{:S(2)}, u32[]{:S(2)}) collective-permute-start(bf16[128,4864]{1,0:T(8,128)(2,1)} %pad_maximum_fusion.1), channel_id=1, source_target_pairs={{0,4},{4,0},{8,12},{12,8},{16,20},{20,16},{24,28},{28,24},{1,5},{5... | collective-permute-start | bytes 3735560 | tf_op jit(solution)/shard_map/ppermute | solution.py:349
  163.9 31.9 %copy-start.6 = (bf16[256,448]{1,0:T(8,128)(2,1)S(1)}, bf16[256,448]{1,0:T(8,128)(2,1)}, u32[]{:S(2)}) copy-start(bf16[256,448]{1,0:T(8,128)(2,1)} %copy-done.5) | copy-start | bytes 688132
  164.0 87.0 %all-gather.10.cloned.1.call-start = ((), (), s32[]{:S(2)}) async-start(), calls=%async_computation.22 | async-start | bytes 3735552 | tf_op jit(solution)/shard_map/all_gather | solution.py:80
  192.2 13.3 %copy-start.2 = (bf16[7,128,256]{1,2,0:T(8,128)(2,1)S(1)}, bf16[7,128,256]{1,2,0:T(8,128)(2,1)}, u32[]{:S(2)}) copy-start(bf16[7,128,256]{1,2,0:T(8,128)(2,1)} %copy-done.1) | copy-start | bytes 1376260
  192.2 67.9 %reduce-scatter.29.cloned.1.call-start = ((), (), s32[]{:S(2)}) async-start(), calls=%async_computation.21 | async-start | bytes 786432 | tf_op jit(solution)/shard_map/reduce_scatter | solution.py:109
  193.1 12.4 %copy-start.32 = (f32[128,64]{0,1:T(8,128)S(1)}, f32[128,64]{0,1:T(8,128)}, u32[]{:S(2)}) copy-start(f32[128,64]{0,1:T(8,128)} %copy-done.31) | copy-start | bytes 98308
  193.1 12.4 %copy-start.25 = (bf16[256,64]{1,0:T(8,128)(2,1)S(1)}, bf16[256,64]{1,0:T(8,128)(2,1)}, u32[]{:S(2)}) copy-start(bf16[256,64]{1,0:T(8,128)(2,1)} %copy-done.24) | copy-start | bytes 98308
  194.1 6.1 %collective-permute-start.6 = (bf16[4,56,256]{2,1,0:T(8,128)(2,1)S(1)}, bf16[4,56,256]{2,1,0:T(8,128)(2,1)S(1)}, u32[]{:S(2)}, u32[]{:S(2)}) collective-permute-start(bf16[4,56,256]{2,1,0:T(8,128)(2,1)S(1)} %get-tuple-element.98), channel_id=1, source_target_pairs={{0,4},{4,0},{8,12},{12,8},{16,20},{20,16},{24,28},{28,24},{1,5},{5... | collective-permute-start | bytes 344072 | tf_op jit(solution)/shard_map/ppermute | solution.py:349
  195.9 8.7 %collective-permute-start.3 = (bf16[256,448]{1,0:T(8,128)(2,1)S(1)}, bf16[256,448]{1,0:T(8,128)(2,1)S(1)}, u32[]{:S(2)}, u32[]{:S(2)}) collective-permute-start(bf16[256,448]{1,0:T(8,128)(2,1)S(1)} %copy-done.6), channel_id=1, source_target_pairs={{0,4},{4,0},{8,12},{12,8},{16,20},{20,16},{24,28},{28,24},{1,5},{5... | collective-permute-start | bytes 688136 | tf_op jit(solution)/shard_map/ppermute | solution.py:349
  206.2 5.3 %copy-start.35 = (bf16[448,64]{1,0:T(8,128)(2,1)S(1)}, bf16[448,64]{1,0:T(8,128)(2,1)}, u32[]{:S(2)}) copy-start(bf16[448,64]{1,0:T(8,128)(2,1)} %copy-done.34) | copy-start | bytes 172036
  211.5 2.6 copy-start.11
  211.5 4.8 %copy-start.4 = (bf16[256,448]{1,0:T(8,128)(2,1)S(1)}, bf16[256,448]{1,0:T(8,128)(2,1)}, u32[]{:S(2)}) copy-start(bf16[256,448]{1,0:T(8,128)(2,1)} %copy-done.3) | copy-start | bytes 688132
  213.8 52.1 %reduce-scatter.17.cloned.1.call-start = ((), (), s32[]{:S(2)}) async-start(), calls=%async_computation.14 | async-start | bytes 786432 | tf_op jit(solution)/shard_map/reduce_scatter | solution.py:109
  214.8 9.1 %collective-permute-start.4 = (bf16[4,56,256]{2,1,0:T(8,128)(2,1)}, bf16[4,56,256]{2,1,0:T(8,128)(2,1)}, u32[]{:S(2)}, u32[]{:S(2)}) collective-permute-start(bf16[4,56,256]{2,1,0:T(8,128)(2,1)} %get-tuple-element.100), channel_id=1, source_target_pairs={{0,4},{4,0},{8,12},{12,8},{16,20},{20,16},{24,28},{28,24},{1,5},{5... | collective-permute-start | bytes 344072 | tf_op jit(solution)/shard_map/ppermute | solution.py:349
  219.6 2.7 copy-start.22
  219.6 4.4 %copy-start.30 = (bf16[4,56,256]{2,1,0:T(8,128)(2,1)S(1)}, bf16[4,56,256]{2,1,0:T(8,128)(2,1)}, u32[]{:S(2)}) copy-start(bf16[4,56,256]{2,1,0:T(8,128)(2,1)} %get-tuple-element.99) | copy-start | bytes 344068
  221.8 19.7 %copy-start.18 = (bf16[256,2432]{1,0:T(8,128)(2,1)S(1)}, bf16[256,2432]{1,0:T(8,128)(2,1)}, u32[]{:S(2)}) copy-start(bf16[256,2432]{1,0:T(8,128)(2,1)} %all-gather.6.cloned.1.call-done) | copy-start | bytes 3735556
  221.8 21.3 %collective-permute-start.2 = (bf16[4,304,256]{2,1,0:T(8,128)(2,1)}, bf16[4,304,256]{2,1,0:T(8,128)(2,1)}, u32[]{:S(2)}, u32[]{:S(2)}) collective-permute-start(bf16[4,304,256]{2,1,0:T(8,128)(2,1)} %get-tuple-element.88), channel_id=1, source_target_pairs={{0,4},{4,0},{8,12},{12,8},{16,20},{20,16},{24,28},{28,24},{1,5},{5... | collective-permute-start | bytes 1867784 | tf_op jit(solution)/shard_map/ppermute | solution.py:349
  222.3 17.9 %collective-permute-start = (bf16[4,56,256]{2,1,0:T(8,128)(2,1)S(1)}, bf16[4,56,256]{2,1,0:T(8,128)(2,1)S(1)}, u32[]{:S(2)}, u32[]{:S(2)}) collective-permute-start(bf16[4,56,256]{2,1,0:T(8,128)(2,1)S(1)} %get-tuple-element.102), channel_id=1, source_target_pairs={{0,4},{4,0},{8,12},{12,8},{16,20},{20,16},{24,28},{28,24},{1,5},{5... | collective-permute-start | bytes 344072 | tf_op jit(solution)/shard_map/ppermute | solution.py:349
  241.0 7.5 %collective-permute-start.5 = (bf16[256,448]{1,0:T(8,128)(2,1)}, bf16[256,448]{1,0:T(8,128)(2,1)}, u32[]{:S(2)}, u32[]{:S(2)}) collective-permute-start(bf16[256,448]{1,0:T(8,128)(2,1)} %all_gather.41), channel_id=1, source_target_pairs={{0,4},{4,0},{8,12},{12,8},{16,20},{20,16},{24,28},{28,24},{1,5},{5... | collective-permute-start | bytes 688136 | tf_op jit(solution)/shard_map/ppermute | solution.py:349
  250.4 7.8 %collective-permute-start.7 = (bf16[256,576]{1,0:T(8,128)(2,1)S(1)}, bf16[256,576]{1,0:T(8,128)(2,1)}, u32[]{:S(2)}, u32[]{:S(2)}) collective-permute-start(bf16[256,576]{1,0:T(8,128)(2,1)S(1)} %all_gather.42), channel_id=1, source_target_pairs={{0,4},{4,0},{8,12},{12,8},{16,20},{20,16},{24,28},{28,24},{1,5},{5... | collective-permute-start | bytes 884744 | tf_op jit(solution)/shard_map/ppermute | solution.py:349
  256.0 4.1 %copy-start.39 = (f32[448]{0:T(512)S(1)}, f32[448]{0:T(512)}, u32[]{:S(2)}) copy-start(f32[448]{0:T(512)} %param.18) | copy-start | bytes 5380
  256.0 4.1 %copy-start.44 = (f32[128]{0:T(128)S(1)}, f32[128]{0:T(128)}, u32[]{:S(2)}) copy-start(f32[128]{0:T(128)} %copy-done.43) | copy-start | bytes 1540
  256.0 5.2 %copy-start.40 = (f32[448]{0:T(512)S(1)}, f32[448]{0:T(512)}, u32[]{:S(2)}) copy-start(f32[448]{0:T(512)} %get-tuple-element.78) | copy-start | bytes 5380
  256.0 9.2 %copy-start.53 = (f32[128]{0:T(128)S(1)}, f32[128]{0:T(128)}, u32[]{:S(2)}) copy-start(f32[128]{0:T(128)} %copy-done.52) | copy-start | bytes 1540
  256.0 9.9 %copy-start.7 = (f32[128,448]{1,0:T(8,128)S(1)}, f32[128,448]{1,0:T(8,128)}, u32[]{:S(2)}) copy-start(f32[128,448]{1,0:T(8,128)} %reduce-scatter.21.cloned.1.call-done) | copy-start | bytes 688132
  256.0 9.9 %copy-start.9 = (bf16[128,448]{1,0:T(8,128)(2,1)S(1)}, bf16[128,448]{1,0:T(8,128)(2,1)}, u32[]{:S(2)}) copy-start(bf16[128,448]{1,0:T(8,128)(2,1)} %copy.150) | copy-start | bytes 344068
  256.0 9.9 %copy-start.38 = (f32[448]{0:T(512)S(1)}, f32[448]{0:T(512)}, u32[]{:S(2)}) copy-start(f32[448]{0:T(512)} %param.26) | copy-start | bytes 5380
  256.0 9.9 %copy-start.42 = (f32[128]{0:T(128)S(1)}, f32[128]{0:T(128)}, u32[]{:S(2)}) copy-start(f32[128]{0:T(128)} %copy-done.41) | copy-start | bytes 1540
  256.1 9.9 %copy-start.46 = (f32[128]{0:T(128)S(1)}, f32[128]{0:T(128)}, u32[]{:S(2)}) copy-start(f32[128]{0:T(128)} %copy-done.45) | copy-start | bytes 1540
  261.3 3.9 %collective-permute-start.8 = (f32[896]{0:T(1024)S(1)}, f32[896]{0:T(1024)S(1)}, u32[]{:S(2)}, u32[]{:S(2)}) collective-permute-start(f32[896]{0:T(1024)S(1)} %pad_maximum_fusion.17), channel_id=1, source_target_pairs={{0,2},{2,0},{1,3},{3,1},{4,6},{6,4},{5,7},{7,5},{8,10},{10,8},{9,1... | collective-permute-start | bytes 10760 | tf_op jit(solution)/shard_map/ppermute | solution.py:512
  265.3 3.7 collective-permute-start.9
  363.2 8.2 %copy-start.23 = (f32[304,448]{1,0:T(8,128)S(1)}, f32[304,448]{1,0:T(8,128)}, u32[]{:S(2)}) copy-start(f32[304,448]{1,0:T(8,128)} %get-tuple-element.154) | copy-start | bytes 1634308
  (13 other events, 15.0 us)
Sparse Core Ops, SparseCore 0:
  23.4 9.5 reduce-scatter.10
  49.4 15.7 reduce-scatter.12
  67.4 10.2 reduce-scatter.18
  82.4 13.6 reduce-scatter.14
  100.9 12.3 all-gather.7
  118.7 15.7 reduce-scatter.20
  148.3 7.8 reduce-scatter.22
  160.4 8.5 reduce-scatter.24
  171.8 8.6 reduce-scatter.26
  182.4 10.4 all-gather.5
  194.4 12.3 all-gather.9
  214.0 15.5 reduce-scatter.28
  243.3 15.5 reduce-scatter.16

commit v2 on v1

--- a/solution.py
+++ b/solution.py
@@ -34,83 +34,8 @@
     cosine = jnp.cos(angle)
     sine = jnp.sin(angle)
     return (
-        jnp.concatenate([cosine, cosine], 1)[:, None, :],
-        jnp.concatenate([sine, sine], 1)[:, None, :],
-    )
-
-
-def rotary(values, cosine, sine):
-    half_width = values.shape[-1] // 2
-    turned = jnp.concatenate([-values[..., half_width:], values[..., :half_width]], -1)
-    return values * cosine + turned * sine
-
-
-def rotary_back(gradient, cosine, sine):
-    turned = gradient * sine
-    half_width = turned.shape[-1] // 2
-    return gradient * cosine + jnp.concatenate(
-        [turned[..., half_width:], -turned[..., :half_width]], -1
-    )
-
-
-def feature_total(values):
-    return lax.psum(values, "col")
-
-
-def norm_forward(values, gain_vector):
-    inverse = lax.rsqrt(feature_total(jnp.sum(values * values, axis=1)) / D + EPSILON)
-    return ((values * inverse[:, None] * gain_vector).astype(jnp.bfloat16), inverse)
-
-
-def norm_backward(gradient, values, inverse, gain_vector):
-    weighted = gradient * gain_vector
-    column_total = feature_total(jnp.sum(weighted * values, axis=1))
-    back_value = (
-        weighted * inverse[:, None]
-        - values * (inverse * inverse * inverse * column_total / D)[:, None]
-    )
-    return (back_value, jnp.sum(gradient * values * inverse[:, None], axis=0))
-
-
-def spread_rows(values):
-    return lax.all_gather(values, "row", axis=0, tiled=True)
-
-
-def spread_cols(values):
-    return lax.all_gather(values, "col", axis=0, tiled=True)
-
-
-def product(left_side, weight, flipped):
-    if flipped:
-        return lax.dot_general(
-            left_side, weight, (((1,), (1,)), ((), ())), preferred_element_type=jnp.float32
-        )
-    return jnp.dot(left_side, weight, preferred_element_type=jnp.float32)
-
-
-def across_columns(gathered, weight, flipped, row_count):
-
-    def partial_term(first_row, how_many):
-        return product(gathered, weight, flipped)
-
-    return lax.psum_scatter(
-        partial_term(jnp.int32(0), lax.axis_size("col") * row_count),
-        "col",
-        scatter_dimension=0,
-        tiled=True,
-    )
-
-
-def across_rows(gathered, weight, flipped, row_count):
-
-    def partial_term(first_row, how_many):
-        return product(gathered, weight, flipped)
-
-    return lax.psum_scatter(
-        partial_term(jnp.int32(0), lax.axis_size("row") * row_count),
-        "row",
-        scatter_dimension=0,
-        tiled=True,
+        jnp.concatenate([cosine, cosine], 1),
+        jnp.concatenate([sine, sine], 1),
     )
 
 
@@ -349,19 +274,347 @@
     return lax.ppermute(values, "dp", [(i, i ^ 1) for i in range(count)])
 
 
-def pair_left(gathered):
+def layer_kernel(
+    tokens, cotangent, gain1, joint, joint_bias, o_weight, gain2, gate_weight, up_weight,
+    down_weight, cosine, sine, allowed,
+    output, input_grad, small_out,
+    first_f, mixed_f, second_f, active_f, cot_f, both_f, branch_f, projected_f,
+    joint_peer, o_peer, gate_peer, up_peer, down_peer, gains_peer,
+    raw_row, raw_send, raw_col, kv, first_oth, second_oth, branch_oth,
+    sum_send, sum_recv, kv_send, kv_recv, out_send, out_recv, send_sem, recv_sem,
+):
+    row, col, pair = lax.axis_index("row"), lax.axis_index("col"), lax.axis_index("dp")
+    row_peer, col_peer = {"row": 1 - row}, {"col": 1 - col}
+    x_peer = {"dp": pair + 1 - 2 * lax.rem(pair, 2)}
+    f32, b16 = jnp.float32, jnp.bfloat16
+    rows, half = tokens.shape
+    width = 2 * half
+    query_width = o_weight.shape[0]
+    key_width = (joint.shape[1] - query_width) // 2
+    heads = query_width // HD
+    hidden_width = gate_weight.shape[1]
+    scale = HD ** (-0.5)
+    started = []
+
+    def copy(source, target, device):
+        at = len(started)
+        made = pltpu.make_async_remote_copy(
+            src_ref=source,
+            dst_ref=target,
+            send_sem=send_sem.at[at],
+            recv_sem=recv_sem.at[at],
+            device_id=device,
+            device_id_type=MESH,
+        )
+        made.start()
+        started.append(made)
+        return made
+
+    def dot(left, right):
+        return jnp.dot(left, right, preferred_element_type=f32)
+
+    def dot_back(left, right):
+        return lax.dot_general(left, right, (((1,), (1,)), ((), ())), preferred_element_type=f32)
+
+    def dot_outer(left, right):
+        return lax.dot_general(left, right, (((0,), (0,)), ((), ())), preferred_element_type=f32)
+
+    barrier = pltpu.get_barrier_semaphore()
+    for device in (row_peer, col_peer, x_peer):
+        pl.semaphore_signal(barrier, inc=1, device_id=device, device_id_type=MESH)
+    pl.semaphore_wait(barrier, 3)
+
+    got_raw = [
+        copy(tokens, raw_row.at[0], row_peer),
+        copy(cotangent, raw_row.at[1], row_peer),
+    ]
+    got_joint = copy(joint, joint_peer, col_peer)
+    gains_peer[0] = gain1[...]
+    gains_peer[1] = gain2[...]
+    got_gains = copy(gains_peer.at[pl.ds(0, 2)], gains_peer.at[pl.ds(2, 2)], col_peer)
+    diagonal = row == col
+    token_own = []
+    got_col = []
+    for i, source in enumerate((tokens, cotangent)):
+        got_raw[i].wait_recv()
+        token_own.append(jnp.where(diagonal, source[...], raw_row[i]))
+        raw_send[i] = jnp.where(diagonal, raw_row[i], source[...])
+        got_col.append(copy(raw_send.at[i], raw_col.at[i], col_peer))
+    got_o = copy(o_weight, o_peer, col_peer)
+    got_gate = copy(gate_weight, gate_peer, col_peer)
+    got_up = copy(up_weight, up_peer, col_peer)
+    got_down = copy(down_weight, down_peer, col_peer)
+    got_gains.wait_recv()
+    gain1_own, gain1_oth = gain1[...], gains_peer[2]
+    gain2_own, gain2_oth = gain2[...], gains_peer[3]
+
+    def total(own, oth):
+        return jnp.sum(own, axis=1, keepdims=True) + jnp.sum(oth, axis=1, keepdims=True)
+
+    def norm_pair(own, oth):
+        return lax.rsqrt(total(own * own, oth * oth) / width + EPSILON)
+
+    later = []
+
+    def split_factor(factor):
+        later.append(copy(factor.at[0], factor.at[2], x_peer))
+        return factor
+
+    def split_rest(factor, got):
+        got.wait_recv()
+        later.append(copy(factor.at[1], factor.at[3], x_peer))
+
+    def shared_factor(factor):
+        later.append(copy(factor.at[0], factor.at[1], col_peer))
+        got = copy(factor.at[0], factor.at[2], x_peer)
+        return got
+
+    def shared_rest(factor, got):
+        got.wait_recv()
+        later.append(copy(factor.at[2], factor.at[3], col_peer))
+
+    tok_own = token_own[0].astype(f32)
+    cot_f[0] = token_own[1]
+    cot_f[1] = raw_send[1]
+    later.append(copy(cot_f.at[pl.ds(0, 2)], cot_f.at[pl.ds(2, 2)], x_peer))
+    got_col[0].wait_recv()
+    tok_oth = raw_col[0].astype(f32)
+    inverse1 = norm_pair(tok_own, tok_oth)
+    first_f[0] = (tok_own * inverse1 * gain1_own).astype(b16)
+    first_oth[...] = (tok_oth * inverse1 * gain1_oth).astype(b16)
+    got_first = copy(first_oth, first_f.at[1], col_peer)
+    split_factor(first_f)
+    got_joint.wait_recv()
+    projected = dot(first_f[0], joint[...]) + dot(first_oth[...], joint_peer[...])
+    projected = projected + joint_bias[...]
+    turn_width = query_width + key_width
+    lane = lax.broadcasted_iota(jnp.int32, (rows, turn_width), 1)
+    first_half = lax.rem(lane, HD) < HD // 2
+
+    def turned(values):
+        return jnp.where(
+            first_half,
+            -pltpu.roll(values, turn_width - HD // 2, 1),
+            pltpu.roll(values, HD // 2, 1),
+        )
+
+    straight = projected[:, :turn_width]
+    spun = (straight * cosine[...] + turned(straight) * sine[...]).astype(b16)
+    kv[0, :, :key_width] = spun[:, query_width:]
+    kv[0, :, key_width:] = projected[:, turn_width:].astype(b16)
+    got_kv = copy(kv.at[0], kv.at[1], col_peer)
+
+    def stack(values):
+        return jnp.concatenate([values[:, h * HD : (h + 1) * HD] for h in range(heads)], 0)
+
+    def unstack(values):
+        return jnp.concatenate([values[h * rows : (h + 1) * rows] for h in range(heads)], 1)
+
+    queries = stack(spun)
+    split_rest(first_f, got_first)
+    got_kv.wait_recv()
+    keys = jnp.concatenate([kv[0, :, :key_width], kv[1, :, :key_width]], 0)
+    values = jnp.concatenate([kv[0, :, key_width:], kv[1, :, key_width:]], 0)
+    mask = jnp.concatenate([allowed[...]] * heads, 0) > 0.5
+    scores = jnp.where(mask, dot_back(queries, keys) * scale, NEGATIVE)
+    raised = jnp.exp(scores - jnp.max(scores, axis=1, keepdims=True))
+    exact = raised / jnp.sum(raised, axis=1, keepdims=True)
+    probs = exact.astype(b16)
+    mixed_f[0] = unstack(dot(probs, values)).astype(b16)
+    got_mixed = shared_factor(mixed_f)
+    got_o.wait_recv()
+
+    def across_rows(at, own, oth):
+        sum_send[at, 0] = own.astype(b16)
+        sum_send[at, 1] = oth.astype(b16)
+        got = copy(sum_send.at[at], sum_recv.at[at], row_peer)
+        return got
+
+    own_part, oth_part = dot(mixed_f[0], o_weight[...]), dot(mixed_f[0], o_peer[...])
+    got = across_rows(0, own_part, oth_part)
+    shared_rest(mixed_f, got_mixed)
+    got_down.wait_recv()
+    got_col[1].wait_recv()
+    grad_activated = dot_back(cot_f[0], down_weight[...]) + dot_back(raw_col[1], down_peer[...])
+    got.wait_recv()
+    hidden_own = tok_own + (own_part + sum_recv[0, 0].astype(f32))
+    hidden_oth = tok_oth + (oth_part + sum_recv[0, 1].astype(f32))
+
+    inverse2 = norm_pair(hidden_own, hidden_oth)
+    second_f[0] = (hidden_own * inverse2 * gain2_own).astype(b16)
+    second_oth[...] = (hidden_oth * inverse2 * gain2_oth).astype(b16)
+    got_second = copy(second_oth, second_f.at[1], col_peer)
+    split_factor(second_f)
+    got_gate.wait_recv()
+    gate_value = dot(second_f[0], gate_weight[...]) + dot(second_oth[...], gate_peer[...])
+    got_up.wait_recv()
+    up_value = dot(second_f[0], up_weight[...]) + dot(second_oth[...], up_peer[...])
+    sigmoid_value = 1.0 / (1.0 + jnp.exp(-gate_value))
+    silu_value = gate_value * sigmoid_value
+    active_f[0] = (silu_value * up_value).astype(b16)
+    grad_gate = (
+        grad_activated * up_value * (sigmoid_value * (1.0 + gate_value * (1.0 - sigmoid_value)))
+    ).astype(b16)
+    grad_up = (grad_activated * silu_value).astype(b16)
+    both_f[0, :, :hidden_width] = grad_gate
+    both_f[0, :, hidden_width:] = grad_up
+    back_own = dot_back(grad_gate, gate_weight[...]) + dot_back(grad_up, up_weight[...])
+    back_oth = dot_back(grad_gate, gate_peer[...]) + dot_back(grad_up, up_peer[...])
+    got_back = across_rows(1, back_own, back_oth)
+    got_both = shared_factor(both_f)
+    got_active = shared_factor(active_f)
+    split_rest(second_f, got_second)
+    out_own, out_oth = dot(active_f[0], down_weight[...]), dot(active_f[0], down_peer[...])
+    got_out = across_rows(2, out_own, out_oth)
+    got_back.wait_recv()
+    back_own = back_own + sum_recv[1, 0].astype(f32)
+    back_oth = back_oth + sum_recv[1, 1].astype(f32)
+
+    def norm_back(grad_own, grad_oth, own, oth, inverse, gain_own, gain_oth):
+        weighted_own, weighted_oth = grad_own * gain_own, grad_oth * gain_oth
+        factor = inverse * inverse * inverse * total(weighted_own * own, weighted_oth * oth) / width
+        return (
+            weighted_own * inverse - own * factor,
+            weighted_oth * inverse - oth * factor,
+            jnp.sum(grad_own * own * inverse, axis=0, keepdims=True),
+            jnp.sum(grad_oth * oth * inverse, axis=0, keepdims=True),
+        )
+
+    hid_own, hid_oth, gain2_part, gain2_rest = norm_back(
+        back_own, back_oth, hidden_own, hidden_oth, inverse2, gain2_own, gain2_oth
+    )
+    hid_own = hid_own + token_own[1].astype(f32)
+    hid_oth = hid_oth + raw_col[1].astype(f32)
+
+    branch_f[0] = hid_own.astype(b16)
+    branch_oth[...] = hid_oth.astype(b16)
+    got_branch = copy(branch_oth, branch_f.at[1], col_peer)
+    split_factor(branch_f)
+    grad_mixed = (
+        dot_back(branch_f[0], o_weight[...]) + dot_back(branch_oth[...], o_peer[...])
+    ).astype(b16)
+    grad_stack = stack(grad_mixed)
+    grad_probs = dot_back(grad_stack, values)
+    grad_scores = exact * (grad_probs - jnp.sum(grad_probs * exact, axis=1, keepdims=True))
+    grad_scores = grad_scores.astype(b16)
+    grad_keys = dot_outer(grad_scores, queries) * scale
+    grad_values = dot_outer(probs, grad_stack)
+    kv_send[:, :key_width] = grad_keys[rows:].astype(b16)
+    kv_send[:, key_width:] = grad_values[rows:].astype(b16)
+    got_kv = copy(kv_send, kv_recv, col_peer)
+    grad_queries = unstack(dot(grad_scores, keys)) * scale
+    split_rest(branch_f, got_branch)
+    got_kv.wait_recv()
+    grad_keys = grad_keys[:rows] + kv_recv[:, :key_width].astype(f32)
+    grad_values = grad_values[:rows] + kv_recv[:, key_width:].astype(f32)
+    turn_grad = jnp.concatenate([grad_queries, grad_keys], 1)
+    turn_grad = turn_grad * cosine[...] - turned(turn_grad * sine[...])
+    projected_f[0] = jnp.concatenate([turn_grad, grad_values], 1).astype(b16)
+    part_own = dot_back(projected_f[0], joint[...])
+    part_oth = dot_back(projected_f[0], joint_peer[...])
+    got_in = across_rows(3, part_own, part_oth)
+    got_projected = shared_factor(projected_f)
+
+    got_out.wait_recv()
+    out_own = hidden_own + (out_own + sum_recv[2, 0].astype(f32))
+    out_oth = hidden_oth + (out_oth + sum_recv[2, 1].astype(f32))
+    out_send[0] = out_oth.astype(b16)
+    got_output = copy(out_send.at[0], out_recv.at[0], col_peer)
+    got_in.wait_recv()
+    part_own = part_own + sum_recv[3, 0].astype(f32)
+    part_oth = part_oth + sum_recv[3, 1].astype(f32)
+    in_own, in_oth, gain1_part, gain1_rest = norm_back(
+        part_own, part_oth, tok_own, tok_oth, inverse1, gain1_own, gain1_oth
+    )
+    in_own = hid_own + in_own
+    in_oth = hid_oth + in_oth
+    out_send[1] = in_oth.astype(b16)
+    got_input = copy(out_send.at[1], out_recv.at[1], col_peer)
+    small_out[0:1, :half] = gain1_part
+    small_out[1:2, :half] = gain1_rest
+    small_out[2:3, :half] = gain2_part
+    small_out[3:4, :half] = gain2_rest
+    small_out[4:5, :] = jnp.sum(projected_f[0].astype(f32), axis=0, keepdims=True)
+    shared_rest(both_f, got_both)
+    shared_rest(active_f, got_active)
+    shared_rest(projected_f, got_projected)
+    got_output.wait_recv()
+    output[...] = jnp.where(diagonal, out_own.astype(b16), out_recv[0])
+    got_input.wait_recv()
+    input_grad[...] = jnp.where(diagonal, in_own.astype(b16), out_recv[1])
+    for made in later:
+        made.wait_recv()
+    for made in started:
+        made.wait_send()
+
+
+def layer_pass(tokens, joint, o_weight, gate_weight, rest):
+    rows, half = tokens.shape
+    query_width, hidden_width, joint_width = o_weight.shape[0], gate_weight.shape[1], joint.shape[1]
+    key_width = (joint_width - query_width) // 2
+    b16, f32 = jnp.bfloat16, jnp.float32
+
+    def blocks(width):
+        return jax.ShapeDtypeStruct((4, rows, width), b16)
+
+    vmem = pl.BlockSpec(memory_space=pltpu.VMEM)
+    outs = [
+        jax.ShapeDtypeStruct((rows, half), b16),
+        jax.ShapeDtypeStruct((rows, half), b16),
+        jax.ShapeDtypeStruct((8, joint_width), f32),
+        blocks(half),
+        blocks(query_width),
+        blocks(half),
+        blocks(hidden_width),
+        blocks(half),
+        blocks(2 * hidden_width),
+        blocks(half),
+        blocks(joint_width),
+    ]
+    return pl.pallas_call(
+        layer_kernel,
+        out_shape=outs,
+        in_specs=[vmem] * len(rest),
+        out_specs=[vmem] * len(outs),
+        scratch_shapes=[
+            pltpu.VMEM((half, joint_width), b16),
+            pltpu.VMEM((query_width, half), b16),
+            pltpu.VMEM((half, hidden_width), b16),
+            pltpu.VMEM((half, hidden_width), b16),
+            pltpu.VMEM((hidden_width, half), b16),
+            pltpu.VMEM((4, 1, half), f32),
+            pltpu.VMEM((2, rows, half), b16),
+            pltpu.VMEM((2, rows, half), b16),
+            pltpu.VMEM((2, rows, half), b16),
+            pltpu.VMEM((2, rows, 2 * key_width), b16),
+            pltpu.VMEM((rows, half), b16),
+            pltpu.VMEM((rows, half), b16),
+            pltpu.VMEM((rows, half), b16),
+            pltpu.VMEM((4, 2, rows, half), b16),
+            pltpu.VMEM((4, 2, rows, half), b16),
+            pltpu.VMEM((rows, 2 * key_width), b16),
+            pltpu.VMEM((rows, 2 * key_width), b16),
+            pltpu.VMEM((2, rows, half), b16),
+            pltpu.VMEM((2, rows, half), b16),
+            pltpu.SemaphoreType.DMA((48,)),
+            pltpu.SemaphoreType.DMA((48,)),
+        ],
+        compiler_params=pltpu.CompilerParams(
+            collective_id=1, has_side_effects=True, vmem_limit_bytes=60 * 1024 * 1024
+        ),
+    )(*rest)
+
+
+def pair_left(blocks):
     line = lax.axis_size("dp") // 2
-    rows, columns = gathered.shape
-    blocks = gathered.T.reshape(line, 2, columns // (2 * line), rows)
-    mine = lax.axis_index("dp") % 2
-    theirs = lax.dynamic_index_in_dim(blocks, 1 - mine, 1, keepdims=False)
-    return jnp.concatenate(
-        [lax.dynamic_index_in_dim(blocks, mine, 1, keepdims=False), swap_pair(theirs)], -1
-    )
-
-
-def pair_right(gathered):
-    return jnp.concatenate([gathered, swap_pair(gathered)], 0)
+    columns = blocks.shape[2]
+    parts = blocks.reshape(-1, line, 2, columns // (2 * line))
+    mine = lax.dynamic_index_in_dim(parts, lax.axis_index("dp") % 2, 2, keepdims=False)
+    return mine.transpose(1, 2, 0)
+
+
+def pair_right(blocks):
+    return blocks.reshape(-1, blocks.shape[2])
 
 
 def per_device(
@@ -386,151 +639,76 @@
     head_rows = group_rows // lax.axis_size("col")
     query_width = q_weight.shape[1]
     key_width = k_weight.shape[1]
-    query_heads = query_width // HD
-    value_heads = key_width // HD
     hidden_width = gate_weight.shape[1]
-    score_scale = HD ** (-0.5)
     places, segment, position = sequence_tables(seq_lengths[0], group_rows)
     block_start = lax.axis_index("col") * head_rows
-    own_places = lax.dynamic_slice_in_dim(places, block_start, head_rows, 0)
-    own_segment = lax.dynamic_slice_in_dim(segment, block_start, head_rows, 0)
-    own_position = lax.dynamic_slice_in_dim(position, block_start, head_rows, 0)
-    allowed = (own_segment[:, None] == segment[None, :]) & (places[None, :] <= own_places[:, None])
-    cosine, sine = rotary_tables(own_position)
-    inputs = tokens.astype(jnp.float32)
-    normed1, inverse1 = norm_forward(inputs, norm1_gain)
-    normed1_all = spread_rows(normed1)
+
+    def from_own(table, how_many):
+        return lax.dynamic_slice_in_dim(jnp.concatenate([table, table]), block_start, how_many, 0)
+
+    own_places, own_segment = from_own(places, head_rows), from_own(segment, head_rows)
+    key_places, key_segment = from_own(places, group_rows), from_own(segment, group_rows)
+    allowed = (own_segment[:, None] == key_segment[None, :]) & (
+        key_places[None, :] <= own_places[:, None]
+    )
+    cosine, sine = rotary_tables(from_own(position, head_rows))
+    turn_heads = (query_width + key_width) // HD
     joint_weight = jnp.concatenate([q_weight, k_weight, v_weight], axis=1)
     joint_bias = jnp.concatenate([q_bias, k_bias, v_bias])
-    projected = across_columns(normed1_all, joint_weight, False, head_rows) + joint_bias
-    queries = rotary(
-        projected[:, :query_width].reshape(head_rows, query_heads, HD), cosine, sine
-    ).astype(jnp.bfloat16)
-    keys_local = rotary(
-        projected[:, query_width : query_width + key_width].reshape(head_rows, value_heads, HD),
-        cosine,
-        sine,
-    ).astype(jnp.bfloat16)
-    values_local = (
-        projected[:, query_width + key_width :]
-        .reshape(head_rows, value_heads, HD)
-        .astype(jnp.bfloat16)
-    )
-    keys_all, values_all = (
-        lax.all_gather(keys_local, "col", axis=0, tiled=True),
-        lax.all_gather(values_local, "col", axis=0, tiled=True),
-    )
-    grouped = queries.reshape(head_rows, value_heads, query_heads // value_heads, HD)
-
-    def score_table():
-        raw_scores = (
-            jnp.einsum("tkgd,skd->kgts", grouped, keys_all, preferred_element_type=jnp.float32)
-            * score_scale
-        )
-        return jnp.where(allowed[None, None], raw_scores, NEGATIVE)
-
-    scores = score_table()
-    highest = jnp.max(scores, axis=-1, keepdims=True)
-    raised = jnp.exp(scores - highest)
-    row_total = jnp.sum(raised, axis=-1, keepdims=True)
-    log_total = highest + jnp.log(row_total)
-    probs = (raised / row_total).astype(jnp.bfloat16)
-    mixed = jnp.einsum("kgts,skd->tkgd", probs, values_all, preferred_element_type=jnp.float32)
-    mixed = mixed.reshape(head_rows, query_width).astype(jnp.bfloat16)
-    mixed_all = spread_cols(mixed)
-    attention = across_rows(mixed_all, o_weight, False, local_rows)
-    hidden = inputs + attention
-    normed2, inverse2 = norm_forward(hidden, norm2_gain)
-    normed2_all = spread_rows(normed2)
-    gate_up = jnp.concatenate([gate_weight, up_weight], axis=1)
-    both_values = across_columns(normed2_all, gate_up, False, head_rows)
-    gate_value = both_values[:, :hidden_width]
-    up_value = both_values[:, hidden_width:]
-    sigmoid_value = jax.nn.sigmoid(gate_value)
-    silu_value = gate_value * sigmoid_value
-    activated = (silu_value * up_value).astype(jnp.bfloat16)
-    activated_all = spread_cols(activated)
-    feed_forward = across_rows(activated_all, down_weight, False, local_rows)
-    output = (hidden + feed_forward).astype(jnp.bfloat16)
-    grad_output_all = spread_rows(cotangent)
-    grad_activated = across_columns(grad_output_all, down_weight, True, head_rows)
-    grad_gate = (
-        grad_activated * up_value * (sigmoid_value * (1.0 + gate_value * (1.0 - sigmoid_value)))
-    )
-    grad_up = grad_activated * silu_value
-    grad_both = jnp.concatenate([grad_gate, grad_up], axis=1).astype(jnp.bfloat16)
-    grad_both_all = spread_cols(grad_both)
-    grad_normed2 = across_rows(grad_both_all, gate_up, True, local_rows)
-    back_second, gain2_part = norm_backward(grad_normed2, hidden, inverse2, norm2_gain)
-    grad_hidden = cotangent.astype(jnp.float32) + back_second
-    grad_branch_all = spread_rows(grad_hidden.astype(jnp.bfloat16))
-    grad_mixed = across_columns(grad_branch_all, o_weight, True, head_rows).astype(jnp.bfloat16)
-    grad_grouped = grad_mixed.reshape(head_rows, value_heads, query_heads // value_heads, HD)
-    probs_again = jnp.exp(score_table() - log_total)
-    grad_probs = jnp.einsum(
-        "tkgd,skd->kgts", grad_grouped, values_all, preferred_element_type=jnp.float32
-    )
-    grad_scores = probs_again * (
-        grad_probs - jnp.sum(grad_probs * probs_again, axis=-1, keepdims=True)
-    )
-    grad_scores = grad_scores.astype(jnp.bfloat16)
-    grad_queries = (
-        jnp.einsum("kgts,skd->tkgd", grad_scores, keys_all, preferred_element_type=jnp.float32)
-        * score_scale
-    )
-    grad_keys_part = (
-        jnp.einsum("kgts,tkgd->skd", grad_scores, grouped, preferred_element_type=jnp.float32)
-        * score_scale
-    )
-    grad_values_part = jnp.einsum(
-        "kgts,tkgd->skd",
-        probs_again.astype(jnp.bfloat16),
-        grad_grouped,
-        preferred_element_type=jnp.float32,
-    )
-    grad_keys, grad_values = (
-        lax.psum_scatter(
-            grad_keys_part.astype(jnp.bfloat16), "col", scatter_dimension=0, tiled=True
-        ).astype(jnp.float32),
-        lax.psum_scatter(
-            grad_values_part.astype(jnp.bfloat16), "col", scatter_dimension=0, tiled=True
-        ).astype(jnp.float32),
-    )
-    grad_q = rotary_back(grad_queries.reshape(head_rows, query_heads, HD), cosine, sine).reshape(
-        head_rows, query_width
-    )
-    grad_k = rotary_back(grad_keys, cosine, sine).reshape(head_rows, key_width)
-    grad_v = grad_values.reshape(head_rows, key_width)
-    grad_projected = jnp.concatenate([grad_q, grad_k, grad_v], axis=1).astype(jnp.bfloat16)
-    grad_projected_all = spread_cols(grad_projected)
-    bias_part = jnp.sum(grad_projected_all, axis=0, dtype=jnp.float32)
-    grad_normed1 = across_rows(grad_projected_all, joint_weight, True, local_rows)
-    back_first, gain1_part = norm_backward(grad_normed1, inputs, inverse1, norm1_gain)
-    input_grad = (grad_hidden + back_first).astype(jnp.bfloat16)
-    def row_pair(values):
-        size = lax.axis_size("row")
-        return values + lax.ppermute(values, "row", [(i, (i + 1) % size) for i in range(size)])
-
+    (
+        output,
+        input_grad,
+        small,
+        first_f,
+        mixed_f,
+        second_f,
+        active_f,
+        cot_f,
+        both_f,
+        branch_f,
+        projected_f,
+    ) = layer_pass(
+        tokens,
+        joint_weight,
+        o_weight,
+        gate_weight,
+        (
+            tokens,
+            cotangent,
+            norm1_gain[None],
+            joint_weight,
+            joint_bias[None],
+            o_weight,
+            norm2_gain[None],
+            gate_weight,
+            up_weight,
+            down_weight,
+            jnp.tile(cosine, (1, turn_heads)),
+            jnp.tile(sine, (1, turn_heads)),
+            allowed.astype(jnp.float32),
+        ),
+    )
+    feature_width = tokens.shape[1]
+    sent = jnp.concatenate([small[1, :feature_width], small[3, :feature_width], small[4]])
+    size = lax.axis_size("col")
+    got = lax.ppermute(sent, "col", [(i, (i + 1) % size) for i in range(size)])
+    kept = jnp.concatenate([small[0, :feature_width], small[2, :feature_width], small[4]])
+    small = kept + got
+    small = small + swap_pair(small)
+    small = jnp.pad(small, (0, -small.shape[0] % 1024)).reshape(-1, 128)
     line = lax.axis_size("dp") // 2
-    feature_width = inputs.shape[1]
-    gains = row_pair(jnp.concatenate([gain1_part, gain2_part]))
-    small = jnp.concatenate([gains, bias_part])
-    small = small + swap_pair(small)
-    small_length = small.shape[0]
-    small = jnp.pad(small, (0, -small_length % 1024)).reshape(-1, 128)
-    rhs_both = jnp.concatenate([grad_both_all, spread_cols(swap_pair(grad_both))], 0)
     padding = ((0, 0), (0, 2 * key_width))
     gate_up_total, down_final, joint_total, small_total = line_totals(
         line,
         (
-            pair_left(normed2_all),
-            rhs_both,
-            pair_left(activated_all),
-            pair_right(grad_output_all),
-            pair_left(mixed_all),
-            jnp.pad(pair_right(grad_branch_all), padding),
-            pair_left(normed1_all),
-            pair_right(grad_projected_all),
+            pair_left(second_f),
+            pair_right(both_f),
+            pair_left(active_f),
+            pair_right(cot_f),
+            pair_left(mixed_f),
+            jnp.pad(pair_right(branch_f), padding),
+            pair_left(first_f),
+            pair_right(projected_f),
             small,
         ),
     )

time: 380 us -> 240 us (0.63)
  waiting for transfers between devices: 114 us -> 0.01 us
  Pallas kernels: 93.6 us -> 193 us
  blocking collectives: 44.9 us -> 0 us
  other arithmetic: 35.9 us -> 4.57 us
  matrix products: 27.7 us -> 0 us
  between operations: 14.7 us -> 0.81 us
  starting transfers between devices: 11.3 us -> 2.1 us
    pallas_call x0 -> x1, Pallas kernels: none -> 98.8 us  [layer_pass(): pl.pallas_call(layer_kernel, out_shape=outs, in_specs=[vmem] * len(rest),...]
    ppermute x9 -> x1, waiting for transfers between devices: 55.9 us -> 0.01 us  [swap_pair(): return lax.ppermute(values, 'dp', [(i, i ^ 1) for i in range(count)])]
    reduce_scatter x10 -> x0, waiting for transfers between devices: 45.8 us -> none  [the longest x4 29.6 us: across_columns(): lax.psum_scatter(partial_term(jnp.int32(0), lax.axis_size('col') * row_co...]
    all_gather x8 -> x0, blocking collectives: 34.9 us -> none  [the longest x4 26.8 us: spread_rows(): return lax.all_gather(values, 'row', axis=0, tiled=True)]
    dot_general x14 -> x0, matrix products: 27.7 us -> none  [the longest x4 11.9 us: product(): lax.dot_general(left_side, weight, (((1,), (1,)), ((), ())), preferred_el...]
    concatenate x14 -> x5, other arithmetic: 17.2 us -> 0.99 us  [the longest x1 0.96 us: per_device(): joint_weight = jnp.concatenate([q_weight, k_weight, v_weight], axis=1)]
    all_gather x3 -> x0, waiting for transfers between devices: 12.5 us -> none  [spread_cols(): return lax.all_gather(values, 'col', axis=0, tiled=True)]
    psum x4 -> x0, blocking collectives: 9.94 us -> none  [feature_total(): return lax.psum(values, 'col')]
  transfers between devices with their start and end apart: 23 -> 2, of which waited for: 13 -> 0; matrix products, arithmetic and copies ran while one was open for 14% -> 7% of each run, Pallas kernels for 0% -> 0%
where the time goes in v2:
time: 240 us; the launch traced here: 239 us
  Pallas kernels  193 us (80%)
  local copies, waits for them, and re-layouts  38.6 us (16%)
  other arithmetic  4.57 us (2%)
    pallas_call x1, Pallas kernels, layer_pass(): pl.pallas_call(layer_kernel, out_shape=outs, in_specs=[vmem] * len(rest),...  98.8 us
    pallas_call x1, Pallas kernels, line_totals(): pl.pallas_call(functools.partial(line_kernel, line), out_shape=[jax.Shape...  94 us
    unnamed x24, local copies, waits for them, and re-layouts  10.4 us
    pallas_call x4, local copies, waits for them, and re-layouts, layer_pass(): pl.pallas_call(layer_kernel, out_shape=outs, in_specs=[vmem] * len(rest),...  6.43 us
  transfers between devices with their start and end apart: 2, of which 0 were waited for; matrix products, arithmetic and copies ran while one was open for 7% of the time, Pallas kernels for 0%

profile of v2, /device:TPU:0, one launch (start us, length us, event | category | flops | bytes accessed | tf_op | source)
XLA Modules:
  0.0 238.8 jit_solution(6020946293903586439)
XLA Ops:
  0.6 0.0 copy-start
  0.7 1.0 reduce-window.4
  1.7 0.7 fusion
  2.3 0.1 convert_reduce_fusion
  2.4 0.1 dynamic_slice.30
  2.5 0.1 dynamic_slice.31
  2.6 0.1 dynamic_slice.33
  2.6 0.1 dynamic_slice.32
  2.7 0.1 select_reduce_fusion
  2.8 0.1 dynamic-slice_convert_fusion
  2.9 0.8 pad_maximum_fusion.3
  3.7 0.6 broadcast_in_dim.21.joint_bias
  4.3 1.0 copy.53
  5.2 1.0 copy.54
  6.2 1.7 copy.55.tokens
  7.9 1.7 copy.56.cotangent
  9.6 0.1 multiply_sine_fusion
  9.7 0.8 copy.58.cosine
  10.6 0.8 copy.59.sine
  11.4 0.0 copy-done
  11.4 2.7 %copy.57.down_weight = bf16[2432,448]{1,0:T(8,128)(2,1)} copy(bf16[2432,448]{0,1:T(8,128)(2,1)S(1)} %copy-done) | data formatting | bytes 4358144 | tf_op args[14]
  14.2 0.0 copy-done.5
  14.2 1.0 pad_maximum_fusion.joint
  15.1 0.7 and_convert_fusion.allowed
  15.9 98.8 %shard_map.254 = (bf16[128,448]{1,0:T(8,128)(2,1)}, bf16[128,448]{1,0:T(8,128)(2,1)}, f32[8,576]{1,0:T(8,128)}, bf16[4,128,448]{2,1,0:T(8,128)(2,1)}, bf16[4,128...) custom-call(bf16[128,448]{1,0:T(8,128)(2,1)} %copy.55.tokens, ...), custom_call_target="tpu_custom_call" | custom-call | tf_op jit(solution)/shard_map/pallas_call | solution.py:574
  114.6 0.0 copy-start.4
  114.7 0.8 slice_reduce_fusion
  115.5 0.9 fusion.4
  116.3 0.1 concatenate.37
  116.4 0.4 collective-permute-start
  116.8 1.3 copy.60
  118.1 0.2 reshape.90
  118.3 0.0 copy-done.4
  118.3 0.3 copy.62
  118.6 0.2 reshape.94
  118.8 4.6 %copy.61 = bf16[4,128,2432]{1,0,2:T(4,128)(2,1)S(1)} copy(bf16[4,128,2432]{2,1,0:T(8,128)(2,1)} %get-tuple-element.33) | data formatting | bytes 4980736 | tf_op jit(solution)/shard_map/pallas_call | solution.py:574
  123.4 2.4 %reshape.92 = bf16[512,4,2,304]{0,3,2,1:T(8,128)(2,1)} reshape(bf16[4,128,2432]{1,0,2:T(4,128)(2,1)S(1)} %copy.61) | data formatting | bytes 4980736 | tf_op jit(solution)/shard_map/reshape | solution.py:611
  125.8 0.7 dynamic-slice_bitcast_fusion.3.lhs_second
  126.5 2.6 %dynamic-slice_bitcast_fusion.lhs_down = bf16[4,304,512]{2,1,0:T(8,128)(2,1)} fusion(bf16[512,4,2,304]{0,3,2,1:T(8,128)(2,1)} %reshape.92, s32[]{:T(128)S(6)} %select_n.35), kind=kLoop, calls=%fused_computation | loop fusion | bytes 2490372 | tf_op jit(solution)/shard_map/transpose | solution.py:613
  129.0 0.7 dynamic-slice_bitcast_fusion.2.lhs_mixed
  129.7 0.0 copy-done.3
  129.7 0.3 copy.63
  130.0 0.2 reshape.96
  130.2 0.1 concatenate.36
  130.3 0.0 collective-permute-done
  130.3 1.7 collective-permute-start.1
  132.0 0.7 dynamic-slice_bitcast_fusion.1.lhs_first
  132.7 0.0 copy-done.7
  132.7 0.8 copy.64
  133.5 0.0 copy-done.6
  133.5 0.8 copy.65
  134.2 0.0 copy-done.2
  134.2 1.0 pad.8.rhs_branch
  135.2 0.0 collective-permute-done.1
  135.2 0.6 pad_bitcast_fusion.small_part
  135.8 94.0 %shard_map.255 = (f32[112,2432]{1,0:T(8,128)}, f32[304,448]{1,0:T(8,128)}, f32[112,576]{1,0:T(8,128)}, f32[16,128]{1,0:T(8,128)}) custom-call(bf16[4,56,512]{2,1,0:T(8,128)(2,1)} %dynamic-slice_bitcast_fusion.3.lhs_second, bf16[512,4864]{1,0:T(8,128)(2,1)} %bitcast.47, bf16[4,304,512]{2,1,0:T(8,128)(2,1)} %dynamic-slice_bitcast_fusion.lhs_down, ...), custom_call_target="tpu_custom_call" | custom-call | tf_op jit(solution)/shard_map/pallas_call | solution.py:250
  229.8 0.0 copy-start.1
  229.9 1.3 fusion.6
  231.2 1.4 fusion.5
  232.6 1.5 fusion.3
  234.1 1.7 fusion.2
  235.7 2.3 fusion.1
  238.0 0.0 copy-done.1
  238.0 0.8 copy.67
  (16 shorter events, 0.1 us)
Async XLA Ops:
  0.6 10.8 %copy-start = (bf16[2432,448]{0,1:T(8,128)(2,1)S(1)}, bf16[2432,448]{0,1:T(8,128)(2,1)}, u32[]{:S(2)}) copy-start(bf16[2432,448]{0,1:T(8,128)(2,1)} %param.29) | copy-start | bytes 6537220
  11.4 2.7 %copy-start.5 = (bf16[448,448]{1,0:T(8,128)(2,1)S(1)}, bf16[448,448]{1,0:T(8,128)(2,1)}, u32[]{:S(2)}) copy-start(bf16[448,448]{1,0:T(8,128)(2,1)} %param.19) | copy-start | bytes 1204228
  114.6 3.7 %copy-start.4 = (bf16[4,128,448]{2,1,0:T(8,128)(2,1)S(1)}, bf16[4,128,448]{2,1,0:T(8,128)(2,1)}, u32[]{:S(2)}) copy-start(bf16[4,128,448]{2,1,0:T(8,128)(2,1)} %get-tuple-element.35) | copy-start | bytes 1376260
  116.4 13.9 %collective-permute-start = (f32[1472]{0:T(1024)S(1)}, f32[1472]{0:T(1024)S(1)}, u32[]{:S(2)}, u32[]{:S(2)}) collective-permute-start(f32[1472]{0:T(1024)S(1)} %concatenate.37), channel_id=1, source_target_pairs={{0,1},{1,0},{2,3},{3,2},{4,5},{5,4},{6,7},{7,6},{8,9},{9,8},{10,11... | collective-permute-start | bytes 17672 | tf_op jit(solution)/shard_map/ppermute | solution.py:694
  125.8 4.0 %copy-start.3 = (bf16[4,128,448]{2,1,0:T(8,128)(2,1)S(1)}, bf16[4,128,448]{2,1,0:T(8,128)(2,1)}, u32[]{:S(2)}) copy-start(bf16[4,128,448]{2,1,0:T(8,128)(2,1)} %get-tuple-element.37) | copy-start | bytes 1376260
  126.5 6.2 %copy-start.7 = (bf16[128,448]{1,0:T(8,128)(2,1)S(1)}, bf16[128,448]{1,0:T(8,128)(2,1)}, u32[]{:S(2)}) copy-start(bf16[128,448]{1,0:T(8,128)(2,1)} %get-tuple-element.72) | copy-start | bytes 344068
  129.0 4.4 %copy-start.6 = (bf16[128,448]{1,0:T(8,128)(2,1)S(1)}, bf16[128,448]{1,0:T(8,128)(2,1)}, u32[]{:S(2)}) copy-start(bf16[128,448]{1,0:T(8,128)(2,1)} %get-tuple-element.73) | copy-start | bytes 344068
  129.0 5.2 %copy-start.2 = (bf16[4,128,448]{2,1,0:T(8,128)(2,1)S(1)}, bf16[4,128,448]{2,1,0:T(8,128)(2,1)}, u32[]{:S(2)}) copy-start(bf16[4,128,448]{2,1,0:T(8,128)(2,1)} %get-tuple-element.36) | copy-start | bytes 1376260
  130.3 4.9 %collective-permute-start.1 = (f32[1472]{0:T(1024)S(1)}, f32[1472]{0:T(1024)S(1)}, u32[]{:S(2)}, u32[]{:S(2)}) collective-permute-start(f32[1472]{0:T(1024)S(1)} %add.35), channel_id=1, source_target_pairs={{0,4},{4,0},{8,12},{12,8},{16,20},{20,16},{24,28},{28,24},{1,5},{5... | collective-permute-start | bytes 17672 | tf_op jit(solution)/shard_map/ppermute | solution.py:274
  229.8 8.2 %copy-start.1 = (f32[304,448]{1,0:T(8,128)S(1)}, f32[304,448]{1,0:T(8,128)}, u32[]{:S(2)}) copy-start(f32[304,448]{1,0:T(8,128)} %get-tuple-element.132) | copy-start | bytes 1634308

commit v3 on v2

--- a/solution.py
+++ b/solution.py
@@ -83,15 +83,30 @@
         def dot(left, right):
             return jnp.dot(left, right, preferred_element_type=jnp.float32)
 
+        def picked(factor):
+            tokens, columns = factor.shape
+            count = columns // (2 * line)
+            shape = (count, columns)
+            first = (2 * target + lax.rem(index, 2)) * count
+            chosen = lax.broadcasted_iota(jnp.int32, shape, 1) == first + lax.broadcasted_iota(
+                jnp.int32, shape, 0
+            )
+            return lax.dot_general(
+                chosen.astype(jnp.float32).astype(jnp.bfloat16),
+                factor[...],
+                (((1,), (1,)), ((), ())),
+                preferred_element_type=jnp.float32,
+            ).astype(jnp.bfloat16)
+
         if piece == 0:
-            left = lhs_second[target]
+            left = picked(lhs_second)
             return jnp.concatenate(
                 [dot(left, rhs_both[:, :hidden_width]), dot(left, rhs_both[:, hidden_width:])], 0
             )
         if piece == 1:
-            return dot(lhs_down[target], rhs_down[...])
+            return dot(picked(lhs_down), rhs_down[...])
         return jnp.concatenate(
-            [dot(lhs_mixed[target], rhs_branch[...]), dot(lhs_first[target], rhs_projected[...])], 0
+            [dot(picked(lhs_mixed), rhs_branch[...]), dot(picked(lhs_first), rhs_projected[...])], 0
         )
 
     outs = (gate_up_out, down_out, joint_out)
@@ -241,9 +256,9 @@
         operands
     )
     shapes = (
-        (2 * lhs_second.shape[1], rhs_both.shape[1] // 2),
-        (lhs_down.shape[1], rhs_down.shape[1]),
-        (2 * lhs_mixed.shape[1], rhs_projected.shape[1]),
+        (lhs_second.shape[1] // line, rhs_both.shape[1] // 2),
+        (lhs_down.shape[1] // (2 * line), rhs_down.shape[1]),
+        (lhs_mixed.shape[1] // line, rhs_projected.shape[1]),
     )
     slots = [pltpu.VMEM((line,) + shape, jnp.bfloat16) for shape in shapes]
     vmem = pl.BlockSpec(memory_space=pltpu.VMEM)
@@ -269,11 +284,6 @@
     )(*operands)
 
 
-def swap_pair(values):
-    count = lax.axis_size("dp")
-    return lax.ppermute(values, "dp", [(i, i ^ 1) for i in range(count)])
-
-
 def layer_kernel(
     tokens, cotangent, gain1, joint, joint_bias, o_weight, gain2, gate_weight, up_weight,
     down_weight, cosine, sine, allowed,
@@ -281,7 +291,7 @@
     first_f, mixed_f, second_f, active_f, cot_f, both_f, branch_f, projected_f,
     joint_peer, o_peer, gate_peer, up_peer, down_peer, gains_peer,
     raw_row, raw_send, raw_col, kv, first_oth, second_oth, branch_oth,
-    sum_send, sum_recv, kv_send, kv_recv, out_send, out_recv, send_sem, recv_sem,
+    sum_send, sum_recv, kv_send, kv_recv, out_send, out_recv, small, small_got, send_sem, recv_sem,
 ):
     row, col, pair = lax.axis_index("row"), lax.axis_index("col"), lax.axis_index("dp")
     row_peer, col_peer = {"row": 1 - row}, {"col": 1 - col}
@@ -530,18 +540,25 @@
     in_oth = hid_oth + in_oth
     out_send[1] = in_oth.astype(b16)
     got_input = copy(out_send.at[1], out_recv.at[1], col_peer)
-    small_out[0:1, :half] = gain1_part
-    small_out[1:2, :half] = gain1_rest
-    small_out[2:3, :half] = gain2_part
-    small_out[3:4, :half] = gain2_rest
-    small_out[4:5, :] = jnp.sum(projected_f[0].astype(f32), axis=0, keepdims=True)
+    bias_part = jnp.sum(projected_f[0].astype(f32), axis=0, keepdims=True)
+    small[...] = jnp.zeros_like(small)
+    for at, parts in ((0, (gain1_rest, gain2_rest)), (1, (gain1_part, gain2_part))):
+        small[at, 0:1, :half] = parts[0]
+        small[at, 1:2, :half] = parts[1]
+        small[at, 2:3, :] = bias_part
+    got_small = copy(small.at[0], small_got.at[0], col_peer)
     shared_rest(both_f, got_both)
     shared_rest(active_f, got_active)
     shared_rest(projected_f, got_projected)
+    got_small.wait_recv()
+    small[2] = small[1] + small_got[0]
+    got_small = copy(small.at[2], small_got.at[1], x_peer)
     got_output.wait_recv()
     output[...] = jnp.where(diagonal, out_own.astype(b16), out_recv[0])
     got_input.wait_recv()
     input_grad[...] = jnp.where(diagonal, in_own.astype(b16), out_recv[1])
+    got_small.wait_recv()
+    small_out[...] = small[2] + small_got[1]
     for made in later:
         made.wait_recv()
     for made in started:
@@ -596,6 +613,8 @@
             pltpu.VMEM((rows, 2 * key_width), b16),
             pltpu.VMEM((2, rows, half), b16),
             pltpu.VMEM((2, rows, half), b16),
+            pltpu.VMEM((3, 8, joint_width), f32),
+            pltpu.VMEM((2, 8, joint_width), f32),
             pltpu.SemaphoreType.DMA((48,)),
             pltpu.SemaphoreType.DMA((48,)),
         ],
@@ -603,14 +622,6 @@
             collective_id=1, has_side_effects=True, vmem_limit_bytes=60 * 1024 * 1024
         ),
     )(*rest)
-
-
-def pair_left(blocks):
-    line = lax.axis_size("dp") // 2
-    columns = blocks.shape[2]
-    parts = blocks.reshape(-1, line, 2, columns // (2 * line))
-    mine = lax.dynamic_index_in_dim(parts, lax.axis_index("dp") % 2, 2, keepdims=False)
-    return mine.transpose(1, 2, 0)
 
 
 def pair_right(blocks):
@@ -689,25 +700,18 @@
         ),
     )
     feature_width = tokens.shape[1]
-    sent = jnp.concatenate([small[1, :feature_width], small[3, :feature_width], small[4]])
-    size = lax.axis_size("col")
-    got = lax.ppermute(sent, "col", [(i, (i + 1) % size) for i in range(size)])
-    kept = jnp.concatenate([small[0, :feature_width], small[2, :feature_width], small[4]])
-    small = kept + got
-    small = small + swap_pair(small)
-    small = jnp.pad(small, (0, -small.shape[0] % 1024)).reshape(-1, 128)
     line = lax.axis_size("dp") // 2
     padding = ((0, 0), (0, 2 * key_width))
     gate_up_total, down_final, joint_total, small_total = line_totals(
         line,
         (
-            pair_left(second_f),
+            pair_right(second_f),
             pair_right(both_f),
-            pair_left(active_f),
+            pair_right(active_f),
             pair_right(cot_f),
-            pair_left(mixed_f),
+            pair_right(mixed_f),
             jnp.pad(pair_right(branch_f), padding),
-            pair_left(first_f),
+            pair_right(first_f),
             pair_right(projected_f),
             small,
         ),
@@ -718,12 +722,10 @@
     query_final = joint_final[:, :query_width]
     key_final = joint_final[:, query_width : query_width + key_width]
     value_final = joint_final[:, query_width + key_width :]
-    small_flat = small_total.reshape(-1)
-    cuts = [feature_width, feature_width, query_width, key_width, key_width]
-    ends = [sum(cuts[: i + 1]) for i in range(len(cuts))]
-    gain1_final, gain2_final, qbias_final, kbias_final, vbias_final = (
-        small_flat[end - cut : end] for end, cut in zip(ends, cuts)
-    )
+    gain1_final, gain2_final = small_total[0, :feature_width], small_total[1, :feature_width]
+    qbias_final = small_total[2, :query_width]
+    kbias_final = small_total[2, query_width : query_width + key_width]
+    vbias_final = small_total[2, query_width + key_width :]
     return (
         output,
         input_grad,

time: 240 us -> 225 us (0.938)
  local copies, waits for them, and re-layouts: 38.6 us -> 23.2 us
  Pallas kernels: 193 us -> 196 us
    pallas_call x4 -> x0, local copies, waits for them, and re-layouts: 6.43 us -> none  [layer_pass(): pl.pallas_call(layer_kernel, out_shape=outs, in_specs=[vmem] * len(rest),...]
    transpose x4 -> x0, local copies, waits for them, and re-layouts: 4.67 us -> none  [pair_left(): return mine.transpose(1, 2, 0)]
    reshape x5 -> x0, local copies, waits for them, and re-layouts: 3.54 us -> none  [the longest x4 2.94 us: pair_left(): parts = blocks.reshape(-1, line, 2, columns // (2 * line))]
    slice x4 -> x1, local copies, waits for them, and re-layouts: 4.44 us -> 1.42 us  [per_device(): small_total[1, :feature_width]]
    unnamed x24 -> x16, local copies, waits for them, and re-layouts: 10.4 us -> 12.2 us
  transfers between devices with their start and end apart: 2 -> 0, of which waited for: 0 -> 0; matrix products, arithmetic and copies ran while one was open for 7% -> 0% of each run, Pallas kernels for 0% -> 0%
where the time goes in v3:
time: 225 us; the launch traced here: 224 us
  Pallas kernels  196 us (87%)
  local copies, waits for them, and re-layouts  23.2 us (10%)
  other arithmetic  4.43 us (2%)
    pallas_call x1, Pallas kernels, layer_pass(): pl.pallas_call(layer_kernel, out_shape=outs, in_specs=[vmem] * len(rest),...  101 us
    pallas_call x1, Pallas kernels, line_totals(): pl.pallas_call(functools.partial(line_kernel, line), out_shape=[jax.Shape...  95 us
    unnamed x16, local copies, waits for them, and re-layouts  12.2 us

profile of v3, /device:TPU:0, one launch (start us, length us, event | category | flops | bytes accessed | tf_op | source)
XLA Modules:
  0.0 224.5 jit_solution(4428091789376528348)
XLA Ops:
  0.6 0.8 reduce-window.4
  1.5 0.7 fusion
  2.1 0.1 convert_reduce_fusion
  2.2 0.1 select_reduce_fusion
  2.3 0.1 dynamic_slice.16
  2.4 0.1 dynamic_slice.17
  2.5 0.1 dynamic-slice_convert_fusion
  2.6 0.1 dynamic_slice.19
  2.7 0.1 dynamic_slice.18
  2.7 0.8 pad_maximum_fusion.3
  3.5 0.6 broadcast_in_dim.21.joint_bias
  4.1 0.1 multiply_sine_fusion
  4.3 1.0 copy.45
  5.2 1.0 copy.46
  6.2 0.0 copy-start.2
  6.2 0.8 and_convert_fusion.allowed
  7.0 1.7 copy.47.tokens
  8.7 1.7 copy.48.cotangent
  10.3 0.0 copy-start
  10.3 0.8 copy.50.cosine
  11.2 0.8 copy.51.sine
  12.0 0.0 copy-done.2
  12.0 1.0 pad_maximum_fusion.joint
  13.0 0.0 copy-done
  13.0 2.8 %copy.49.down_weight = bf16[2432,448]{1,0:T(8,128)(2,1)} copy(bf16[2432,448]{0,1:T(8,128)(2,1)S(1)} %copy-done) | data formatting | bytes 4358144 | tf_op args[14]
  15.8 101.1 %shard_map.254 = (bf16[128,448]{1,0:T(8,128)(2,1)}, bf16[128,448]{1,0:T(8,128)(2,1)}, f32[8,576]{1,0:T(8,128)}, bf16[4,128,448]{2,1,0:T(8,128)(2,1)}, bf16[4,128...) custom-call(bf16[128,448]{1,0:T(8,128)(2,1)} %copy.47.tokens, ...), custom_call_target="tpu_custom_call" | custom-call | tf_op jit(solution)/shard_map/pallas_call | solution.py:591
  116.8 1.7 copy.52
  118.5 1.7 copy.53
  120.2 2.0 pad.4.rhs_branch
  122.2 95.0 %shard_map.255 = (f32[112,2432]{1,0:T(8,128)}, f32[304,448]{1,0:T(8,128)}, f32[112,576]{1,0:T(8,128)}, f32[8,576]{1,0:T(8,128)}) custom-call(bf16[512,448]{1,0:T(8,128)(2,1)} %bitcast.34, bf16[512,4864]{1,0:T(8,128)(2,1)} %bitcast.27, bf16[512,2432]{1,0:T(8,128)(2,1)} %bitcast.28, bf16[512,448]{1,0:T(8,128)(2,1)} %bitcast.35, bf16[512,448]{1,0:T(8,128)(2,1)} %bitcast.33, ...), custom_call_target="tpu_custom_call" | custom-call | tf_op jit(solution)/shard_map/pallas_call | solution.py:265
  217.2 0.0 copy-start.3
  217.2 0.0 copy-start.1
  217.2 2.3 %fusion.1 = (f32[56,2432]{1,0:T(8,128)}, f32[56,2432]{1,0:T(8,128)}) fusion(f32[112,2432]{1,0:T(8,128)} %get-tuple-element.42), kind=kLoop, calls=%fused_computation.21 | loop fusion | bytes 2179072 | tf_op jit(solution)/shard_map/slice | solution.py:720
  219.6 1.3 slice_bitcast_fusion
  220.8 1.4 fusion.4
  222.3 0.0 copy-done.3
  222.3 0.7 fusion.3
  223.0 0.7 fusion.2
  223.7 0.0 copy-done.1
  223.7 0.8 copy.55
  (9 shorter events, 0.1 us)
Async XLA Ops:
  6.2 5.8 %copy-start.2 = (bf16[448,448]{1,0:T(8,128)(2,1)S(1)}, bf16[448,448]{1,0:T(8,128)(2,1)}, u32[]{:S(2)}) copy-start(bf16[448,448]{1,0:T(8,128)(2,1)} %param.19) | copy-start | bytes 1204228
  10.3 2.7 %copy-start = (bf16[2432,448]{0,1:T(8,128)(2,1)S(1)}, bf16[2432,448]{0,1:T(8,128)(2,1)}, u32[]{:S(2)}) copy-start(bf16[2432,448]{0,1:T(8,128)(2,1)} %param.29) | copy-start | bytes 6537220
  217.2 5.1 %copy-start.3 = (f32[112,576]{1,0:T(8,128)S(1)}, f32[112,576]{1,0:T(8,128)}, u32[]{:S(2)}) copy-start(f32[112,576]{1,0:T(8,128)} %get-tuple-element.41) | copy-start | bytes 774148
  217.2 6.4 %copy-start.1 = (f32[304,448]{1,0:T(8,128)S(1)}, f32[304,448]{1,0:T(8,128)}, u32[]{:S(2)}) copy-start(f32[304,448]{1,0:T(8,128)} %get-tuple-element.128) | copy-start | bytes 1634308
